TPU v7x, 32 devices: a whole 2x2x4 slice. The times are simulated.
32 devices in a mesh: groups: 2 (over y), expert: 8 (over z, core), dp: 2 (over x).
Axes of the slice: x: 2, y: 2, z: 4, core: 2. Of those that a mesh axis runs over, the one named last changes fastest.
Arguments:
- tokens: bfloat16 [768, 2048], P(('groups', 'expert', 'dp')), parts along dimension 0, may hold values from -6 to 6
- cotangent: bfloat16 [768, 2048], P(('groups', 'expert', 'dp')), parts along dimension 0, may hold values from -6 to 6
- routes: int32 [768, 6], P(('groups', 'expert', 'dp')), parts along dimension 0, may hold values from 0 to 15, all different within a row; in each aligned block of 24 rows (0 to 23, 24 to 47, ...) at most 11 rows name the same one
- mix_weights: bfloat16 [768, 6], P(('groups', 'expert', 'dp')), parts along dimension 0, may hold values from 0.049804688 to 0.5
- gate_matrix: bfloat16 [2048, 16384], P(None, ('expert', 'dp')), may hold values from -0.125 to 0.125
- up_matrix: bfloat16 [2048, 16384], P(None, ('expert', 'dp')), may hold values from -0.125 to 0.125
- down_matrix: bfloat16 [16384, 2048], P(('expert', 'dp')), may hold values from -0.1875 to 0.1875
Outputs:
- grad_tokens: bfloat16 [768, 2048], P(('groups', 'expert', 'dp')), parts along dimension 0
- grad_mix: float32 [768, 6], P(('groups', 'expert', 'dp')), parts along dimension 0
- grad_gate: float32 [2048, 32768], P(None, ('groups', 'expert', 'dp')), parts along dimension 1
- grad_up: float32 [2048, 32768], P(None, ('groups', 'expert', 'dp')), parts along dimension 1
- grad_down: float32 [32768, 2048], P(('groups', 'expert', 'dp')), parts along dimension 0
There are 2 independent parts, one for each index of `groups`. A program takes and returns all parts, laid end to end along the dimension named above; an argument that names none is the same for every part. Nothing has to cross between parts.
Inputs may be any that keep to these rules, and one draw needn't show every extreme that they name: `routes`: each row names 6 different experts. In each aligned block of 24 rows (the tokens of one device) no expert is named more than 11 times, a bound that some block reaches.
All inputs are finite; a program needn't handle non-finite values.
Results may differ from a plain program's by a relative error of at most 0.0085.
Values may be sent and summed in bfloat16 or wider, within the bound.
A program may use at most 128 MiB of HBM per device.

v0:
```python
import jax
import jax.numpy as jnp
from jax import lax
from jax.sharding import PartitionSpec as P


def expert_backward(row_tokens, row_cotan, row_mix, gate_matrix, up_matrix, down_matrix):
    contract_last = (((1,), (1,)), ((), ()))
    contract_first = (((0,), (0,)), ((), ()))
    pre_gate = jnp.dot(row_tokens, gate_matrix, preferred_element_type=jnp.float32)
    pre_up = jnp.dot(row_tokens, up_matrix, preferred_element_type=jnp.float32)
    sigmoid_gate = jax.nn.sigmoid(pre_gate)
    activated = pre_gate * sigmoid_gate
    hidden = (activated * pre_up).astype(jnp.bfloat16)
    back_hidden = lax.dot_general(
        row_cotan, down_matrix, contract_last, preferred_element_type=jnp.float32
    )
    mix_column = row_mix.astype(jnp.float32)[:, None]
    scaled_cotan = (mix_column * row_cotan.astype(jnp.float32)).astype(jnp.bfloat16)
    grad_hidden = mix_column * back_hidden
    grad_upper = (grad_hidden * activated).astype(jnp.bfloat16)
    grad_pregate = (
        grad_hidden * pre_up * sigmoid_gate * (1.0 + pre_gate * (1.0 - sigmoid_gate))
    ).astype(jnp.bfloat16)
    mix_partial = jnp.sum(hidden.astype(jnp.float32) * back_hidden, axis=1).astype(jnp.bfloat16)
    down_grad = lax.dot_general(
        hidden, scaled_cotan, contract_first, preferred_element_type=jnp.float32
    )
    gate_grad = lax.dot_general(
        row_tokens, grad_pregate, contract_first, preferred_element_type=jnp.float32
    )
    up_grad = lax.dot_general(
        row_tokens, grad_upper, contract_first, preferred_element_type=jnp.float32
    )
    joined_grad = jnp.concatenate([grad_pregate, grad_upper], axis=1)
    joined_weight = jnp.concatenate([gate_matrix, up_matrix], axis=1)
    token_partial = lax.dot_general(
        joined_grad, joined_weight, contract_last, preferred_element_type=jnp.float32
    ).astype(jnp.bfloat16)
    return (token_partial, mix_partial, gate_grad, up_grad, down_grad)


def local(tokens, cotangent, routes, mix_weights, gate_matrix, up_matrix, down_matrix):
    tok_count, features = tokens.shape
    top_count = routes.shape[1]
    columns = lax.axis_size("expert")
    dp_size = lax.axis_size("dp")
    team_size = dp_size // 2
    experts = 2 * columns
    slot_most = min(5 * tok_count * top_count // (4 * experts), tok_count)
    row_count = tok_count * top_count
    slot_count = experts * slot_most
    expert_ids = routes.reshape(row_count)
    onehot = (expert_ids[:, None] == jnp.arange(experts, dtype=jnp.int32)[None, :]).astype(
        jnp.bfloat16
    )
    row_index = jnp.arange(row_count, dtype=jnp.int32)
    earlier = (row_index[None, :] < row_index[:, None]).astype(jnp.bfloat16)
    prior_count = jnp.dot(earlier, onehot, preferred_element_type=jnp.float32)
    position = jnp.sum(prior_count * onehot.astype(jnp.float32), axis=1).astype(jnp.int32)
    slot_ids = expert_ids * slot_most + position
    slot_pick = (slot_ids[:, None] == jnp.arange(slot_count, dtype=jnp.int32)[None, :]).astype(
        jnp.bfloat16
    )
    token_rows = jnp.repeat(tokens, top_count, axis=0)
    cotan_rows = jnp.repeat(cotangent, top_count, axis=0)
    mix_rows = mix_weights.reshape(row_count, 1)
    pick_form = "rs,rd->sd"
    token_slots = jnp.einsum(
        pick_form, slot_pick, token_rows, preferred_element_type=jnp.float32
    ).astype(jnp.bfloat16)
    cotan_slots = jnp.einsum(
        pick_form, slot_pick, cotan_rows, preferred_element_type=jnp.float32
    ).astype(jnp.bfloat16)
    mix_slots = (
        jnp.einsum(pick_form, slot_pick, mix_rows, preferred_element_type=jnp.float32)
        .astype(jnp.bfloat16)
        .reshape(slot_count)
    )

    def spread(values):
        rest = values.shape[1:]
        lead = values.reshape((columns, 2, 1, slot_most) + rest)
        wide = jnp.broadcast_to(lead, (columns, 2, team_size, slot_most) + rest)
        return wide.reshape((columns, dp_size, slot_most) + rest)

    arrived = (
        lax.all_to_all(
            lax.all_to_all(spread(token_slots), "expert", split_axis=0, concat_axis=0, tiled=True),
            "dp",
            split_axis=1,
            concat_axis=1,
            tiled=True,
        ),
        lax.all_to_all(
            lax.all_to_all(spread(cotan_slots), "expert", split_axis=0, concat_axis=0, tiled=True),
            "dp",
            split_axis=1,
            concat_axis=1,
            tiled=True,
        ),
        lax.all_to_all(
            lax.all_to_all(spread(mix_slots), "expert", split_axis=0, concat_axis=0, tiled=True),
            "dp",
            split_axis=1,
            concat_axis=1,
            tiled=True,
        ),
    )
    token_partial, mix_partial, gate_grad, up_grad, down_grad = expert_backward(
        arrived[0].reshape(-1, features),
        arrived[1].reshape(-1, features),
        arrived[2].reshape(-1),
        gate_matrix,
        up_matrix,
        down_matrix,
    )
    returned = (
        lax.all_to_all(
            lax.all_to_all(
                token_partial.reshape(columns, dp_size, slot_most, features),
                "expert",
                split_axis=0,
                concat_axis=0,
                tiled=True,
            ),
            "dp",
            split_axis=1,
            concat_axis=1,
            tiled=True,
        ),
        lax.all_to_all(
            lax.all_to_all(
                mix_partial.reshape(columns, dp_size, slot_most),
                "expert",
                split_axis=0,
                concat_axis=0,
                tiled=True,
            ),
            "dp",
            split_axis=1,
            concat_axis=1,
            tiled=True,
        ),
    )
    token_sums = (
        returned[0]
        .reshape(columns, 2, team_size, slot_most, features)
        .astype(jnp.float32)
        .sum(axis=2)
        .reshape(slot_count, features)
    )
    mix_sums = (
        returned[1]
        .reshape(columns, 2, team_size, slot_most)
        .astype(jnp.float32)
        .sum(axis=2)
        .reshape(slot_count)
    )
    token_pick = slot_pick.reshape(tok_count, top_count, slot_count).astype(jnp.float32).sum(axis=1)
    grad_tokens = jnp.dot(token_pick, token_sums, precision=lax.Precision.HIGHEST).astype(
        jnp.bfloat16
    )
    grad_mix = jnp.dot(
        slot_pick.astype(jnp.float32), mix_sums[:, None], precision=lax.Precision.HIGHEST
    ).reshape(tok_count, top_count)
    return (grad_tokens, grad_mix, gate_grad, up_grad, down_grad)


def solution(mesh):
    in_specs = (
        P(("groups", "expert", "dp"), None),
        P(("groups", "expert", "dp"), None),
        P(("groups", "expert", "dp"), None),
        P(("groups", "expert", "dp"), None),
        P(None, ("expert", "dp")),
        P(None, ("expert", "dp")),
        P(("expert", "dp"), None),
    )
    out_specs = (
        P(("groups", "expert", "dp"), None),
        P(("groups", "expert", "dp"), None),
        P(None, ("groups", "expert", "dp")),
        P(None, ("groups", "expert", "dp")),
        P(("groups", "expert", "dp"), None),
    )
    return jax.shard_map(local, mesh=mesh, in_specs=in_specs, out_specs=out_specs, check_vma=False)
```

profile of v0, /device:TPU:1, one launch (start us, length us, event | category | flops | bytes accessed | tf_op | source)
XLA Modules:
  0.0 161.4 jit_solution(10062682924691273398)
XLA Ops:
  3.5 6.4 %all-to-all-start = ((bf16[8,2,11]{2,1,0:T(2,128)(2,1)}), bf16[8,2,11]{2,1,0:T(2,128)(2,1)S(1)}, u32[]{:S(2)}, u32[]{:S(2)}) async-start(bf16[8,2,11]{2,1,0:T(2,128)(2,1)} %reshape_reshape_reshape.3), calls=%async_computation | async-start | bytes 8192 | tf_op jit(solution)/shard_map/all_to_all | solution.py:103
  11.1 3.5 %all-to-all-done = bf16[8,2,11]{2,1,0:T(2,128)(2,1)S(1)} async-done(((bf16[8,2,11]{2,1,0:T(2,128)(2,1)}), bf16[8,2,11]{2,1,0:T(2,128)(2,1)S(1)}, u32[]{:S(2)}, u32[]{:S(2)}) %all-to-all-start) | async-done | bytes 384 | tf_op jit(solution)/shard_map/all_to_all | solution.py:103
  15.2 3.2 %all-to-all-start.1 = ((bf16[8,2,11]{2,0,1:T(8,128)(2,1)}), bf16[8,2,11]{2,0,1:T(8,128)(2,1)S(1)}, u32[]{:S(2)}, u32[]{:S(2)}) async-start(bf16[8,2,11]{2,0,1:T(8,128)(2,1)} %copy.69), calls=%async_computation.1 | async-start | bytes 8192 | tf_op jit(solution)/shard_map/all_to_all | solution.py:102
  21.1 5.3 %all-to-all-start.4 = ((bf16[8,2,11,2048]{3,1,2,0:T(2,128)(2,1)}), bf16[8,2,11,2048]{3,1,2,0:T(2,128)(2,1)S(1)}, u32[]{:S(2)}, u32[]{:S(2)}) async-start(bf16[8,2,11,2048]{3,1,2,0:T(2,128)(2,1)} %copy.74), calls=%async_computation.4 | async-start | bytes 1441792 | tf_op jit(solution)/shard_map/all_to_all | solution.py:89
  29.1 16.0 %all-to-all-done.4 = bf16[8,2,11,2048]{3,1,2,0:T(2,128)(2,1)S(1)} async-done(((bf16[8,2,11,2048]{3,1,2,0:T(2,128)(2,1)}), bf16[8,2,11,2048]{3,1,2,0:T(2,128)(2,1)S(1)}, u32[]{:S(2)}, u32[]{:S(2)}) %all-to-all-start.4) | async-done | bytes 720928 | tf_op jit(solution)/shard_map/all_to_all | solution.py:89
  45.1 4.3 %all-to-all-start.2 = ((bf16[8,2,11,2048]{3,1,2,0:T(2,128)(2,1)}), bf16[8,2,11,2048]{3,1,2,0:T(2,128)(2,1)S(1)}, u32[]{:S(2)}, u32[]{:S(2)}) async-start(bf16[8,2,11,2048]{3,1,2,0:T(2,128)(2,1)} %copy.71), calls=%async_computation.2 | async-start | bytes 1441792 | tf_op jit(solution)/shard_map/all_to_all | solution.py:96
  50.5 17.6 %all-to-all-done.2 = bf16[8,2,11,2048]{3,1,2,0:T(2,128)(2,1)S(1)} async-done(((bf16[8,2,11,2048]{3,1,2,0:T(2,128)(2,1)}), bf16[8,2,11,2048]{3,1,2,0:T(2,128)(2,1)S(1)}, u32[]{:S(2)}, u32[]{:S(2)}) %all-to-all-start.2) | async-done | bytes 720928 | tf_op jit(solution)/shard_map/all_to_all | solution.py:96
  68.2 3.5 %all-to-all-start.5 = ((bf16[8,2,11,2048]{3,0,2,1:T(8,128)(2,1)}), bf16[8,2,11,2048]{3,0,2,1:T(8,128)(2,1)S(1)}, u32[]{:S(2)}, u32[]{:S(2)}) async-start(bf16[8,2,11,2048]{3,0,2,1:T(8,128)(2,1)} %copy.75), calls=%async_computation.5 | async-start | bytes 1441792 | tf_op jit(solution)/shard_map/all_to_all | solution.py:88
  72.9 8.0 %all-to-all-done.5 = bf16[8,2,11,2048]{3,0,2,1:T(8,128)(2,1)S(1)} async-done(((bf16[8,2,11,2048]{3,0,2,1:T(8,128)(2,1)}), bf16[8,2,11,2048]{3,0,2,1:T(8,128)(2,1)S(1)}, u32[]{:S(2)}, u32[]{:S(2)}) %all-to-all-start.5) | async-done | bytes 720928 | tf_op jit(solution)/shard_map/all_to_all | solution.py:88
  81.0 3.5 %all-to-all-start.3 = ((bf16[8,2,11,2048]{3,0,2,1:T(8,128)(2,1)}), bf16[8,2,11,2048]{3,0,2,1:T(8,128)(2,1)S(1)}, u32[]{:S(2)}, u32[]{:S(2)}) async-start(bf16[8,2,11,2048]{3,0,2,1:T(8,128)(2,1)} %copy.72), calls=%async_computation.3 | async-start | bytes 1441792 | tf_op jit(solution)/shard_map/all_to_all | solution.py:95
  85.2 3.3 %fusion.27 = f32[176,1024]{1,0:T(8,128)S(1)} fusion(bf16[176,2048]{1,0:T(8,128)(2,1)S(1)} %reshape.111, bf16[2048,1024]{1,0:T(8,128)(2,1)} %param.11), kind=kOutput, calls=%fused_computation.42 | convolution fusion | flops 738197504 | bytes 5636096 | tf_op jit(solution)/shard_map/dot_general | solution.py:10
  88.7 1.8 %fusion.26 = f32[176,1024]{1,0:T(8,128)} fusion(bf16[176,2048]{1,0:T(8,128)(2,1)S(1)} %reshape.111, bf16[2048,1024]{1,0:T(8,128)(2,1)S(1)} %copy-done), kind=kOutput, calls=%fused_computation.41 | convolution fusion | flops 738197504 | bytes 5636096 | tf_op jit(solution)/shard_map/dot_general | solution.py:11
  90.5 2.3 %all-to-all-done.3 = bf16[8,2,11,2048]{3,0,2,1:T(8,128)(2,1)S(1)} async-done(((bf16[8,2,11,2048]{3,0,2,1:T(8,128)(2,1)}), bf16[8,2,11,2048]{3,0,2,1:T(8,128)(2,1)S(1)}, u32[]{:S(2)}, u32[]{:S(2)}) %all-to-all-start.3) | async-done | bytes 720928 | tf_op jit(solution)/shard_map/all_to_all | solution.py:95
  93.5 5.1 %multiply_reduce_fusion = (bf16[176]{0:T(256)(128)(2,1)S(1)}, bf16[176,1024]{1,0:T(8,128)(2,1)}, bf16[176,1024]{1,0:T(8,128)(2,1)}, bf16[176,1024]{1,0:T(8,128)(2,1)}) fusion(f32[176,1024]{1,0:T(8,128)} %fusion.26, f32[176,1024]{1,0:T(8,128)S(1)} %fusion.27, f32[176]{0:T(256)S(1)} %reshape.115, bf16[176,2048]{1,0:T(8,128)(2,1)S(1)} %reshape.109, ...), kind=kOutput, calls=%fused_computation.16 | convolution fusion | flops 741621568 | bytes 7439392 | tf_op jit(solution)/shard_map/dot_general | solution.py:15
  99.4 6.1 %all-to-all-start.8 = ((bf16[8,2,11]{2,1,0:T(2,128)(2,1)}), bf16[8,2,11]{2,1,0:T(2,128)(2,1)S(1)}, u32[]{:S(2)}, u32[]{:S(2)}) async-start(bf16[8,2,11]{2,1,0:T(2,128)(2,1)} %convert_element_type.97), calls=%async_computation.8 | async-start | bytes 8192 | tf_op jit(solution)/shard_map/all_to_all | solution.py:133
  105.5 6.6 %fusion.4 = bf16[176,2048]{1,0:T(8,128)(2,1)S(1)} fusion(bf16[2048,1024]{1,0:T(8,128)(2,1)} %param.12, bf16[2048,1024]{1,0:T(8,128)(2,1)} %param.11, bf16[176,1024]{1,0:T(8,128)(2,1)} %get-tuple-element.8, bf16[176,1024]{1,0:T(8,128)(2,1)} %get-tuple-element.7), kind=kOutput, calls=%fused_computation.4 | convolution fusion | flops 1494974464 | bytes 9830400 | tf_op jit(solution)/shard_map/dot_general | solution.py:37
  114.0 5.1 %all-to-all-start.6 = ((bf16[8,2,11,2048]{3,1,2,0:T(2,128)(2,1)}), bf16[8,2,11,2048]{3,1,2,0:T(2,128)(2,1)S(1)}, u32[]{:S(2)}, u32[]{:S(2)}) async-start(bf16[8,2,11,2048]{3,1,2,0:T(2,128)(2,1)} %copy.77), calls=%async_computation.6 | async-start | bytes 1441792 | tf_op jit(solution)/shard_map/all_to_all | solution.py:120
  119.4 5.8 %fusion.8 = f32[1024,2048]{1,0:T(8,128)} fusion(bf16[176,1024]{1,0:T(8,128)(2,1)} %get-tuple-element.6, bf16[176,2048]{1,0:T(8,128)(2,1)S(1)} %reshape.109, f32[176]{0:T(256)S(1)} %reshape.115), kind=kOutput, calls=%fused_computation.11 | convolution fusion | flops 739278848 | bytes 9470656 | tf_op jit(solution)/shard_map/dot_general | solution.py:26
  125.8 12.0 %all-to-all-done.6 = bf16[8,2,11,2048]{3,1,2,0:T(2,128)(2,1)S(1)} async-done(((bf16[8,2,11,2048]{3,1,2,0:T(2,128)(2,1)}), bf16[8,2,11,2048]{3,1,2,0:T(2,128)(2,1)S(1)}, u32[]{:S(2)}, u32[]{:S(2)}) %all-to-all-start.6) | async-done | bytes 720928 | tf_op jit(solution)/shard_map/all_to_all | solution.py:120
  137.8 3.2 %all-to-all-start.9 = ((bf16[8,2,11]{2,0,1:T(8,128)(2,1)}), bf16[8,2,11]{2,0,1:T(8,128)(2,1)S(1)}, u32[]{:S(2)}, u32[]{:S(2)}) async-start(bf16[8,2,11]{2,0,1:T(8,128)(2,1)} %copy.80), calls=%async_computation.9 | async-start | bytes 8192 | tf_op jit(solution)/shard_map/all_to_all | solution.py:132
  141.1 4.7 %fusion.28 = f32[2048,1024]{1,0:T(8,128)} fusion(bf16[176,2048]{1,0:T(8,128)(2,1)S(1)} %reshape.111, bf16[176,1024]{1,0:T(8,128)(2,1)S(1)} %copy-done.2), kind=kOutput, calls=%fused_computation.43 | convolution fusion | flops 738197504 | bytes 9469952 | tf_op jit(solution)/shard_map/dot_general | solution.py:29
  146.9 3.5 %all-to-all-start.7 = ((bf16[8,2,11,2048]{3,0,2,1:T(8,128)(2,1)}), bf16[8,2,11,2048]{3,0,2,1:T(8,128)(2,1)S(1)}, u32[]{:S(2)}, u32[]{:S(2)}) async-start(bf16[8,2,11,2048]{3,0,2,1:T(8,128)(2,1)} %copy.78), calls=%async_computation.7 | async-start | bytes 1441792 | tf_op jit(solution)/shard_map/all_to_all | solution.py:119
  150.4 4.7 %fusion.29 = f32[2048,1024]{1,0:T(8,128)} fusion(bf16[176,2048]{1,0:T(8,128)(2,1)S(1)} %reshape.111, bf16[176,1024]{1,0:T(8,128)(2,1)S(1)} %copy-done.1), kind=kOutput, calls=%fused_computation.44 | convolution fusion | flops 738197504 | bytes 9469952 | tf_op jit(solution)/shard_map/dot_general | solution.py:32
  156.2 3.5 %all-to-all-done.7 = bf16[8,2,11,2048]{3,0,2,1:T(8,128)(2,1)S(1)} async-done(((bf16[8,2,11,2048]{3,0,2,1:T(8,128)(2,1)}), bf16[8,2,11,2048]{3,0,2,1:T(8,128)(2,1)S(1)}, u32[]{:S(2)}, u32[]{:S(2)}) %all-to-all-start.7) | async-done | bytes 720928 | tf_op jit(solution)/shard_map/all_to_all | solution.py:119
  (58 shorter events, 21.2 us)
Async XLA Ops:
  3.5 11.2 %all-to-all-start = ((bf16[8,2,11]{2,1,0:T(2,128)(2,1)}), bf16[8,2,11]{2,1,0:T(2,128)(2,1)S(1)}, u32[]{:S(2)}, u32[]{:S(2)}) async-start(bf16[8,2,11]{2,1,0:T(2,128)(2,1)} %reshape_reshape_reshape.3), calls=%async_computation | async-start | bytes 8192 | tf_op jit(solution)/shard_map/all_to_all | solution.py:103
  9.9 16.5 %copy-start.3 = (bf16[24,2048]{1,0:T(8,128)(2,1)S(1)}, bf16[24,2048]{1,0:T(8,128)(2,1)}, u32[]{:S(2)}) copy-start(bf16[24,2048]{1,0:T(8,128)(2,1)} %param.8) | copy-start | bytes 294916
  15.2 5.9 %all-to-all-start.1 = ((bf16[8,2,11]{2,0,1:T(8,128)(2,1)}), bf16[8,2,11]{2,0,1:T(8,128)(2,1)S(1)}, u32[]{:S(2)}, u32[]{:S(2)}) async-start(bf16[8,2,11]{2,0,1:T(8,128)(2,1)} %copy.69), calls=%async_computation.1 | async-start | bytes 8192 | tf_op jit(solution)/shard_map/all_to_all | solution.py:102
  21.1 24.0 %all-to-all-start.4 = ((bf16[8,2,11,2048]{3,1,2,0:T(2,128)(2,1)}), bf16[8,2,11,2048]{3,1,2,0:T(2,128)(2,1)S(1)}, u32[]{:S(2)}, u32[]{:S(2)}) async-start(bf16[8,2,11,2048]{3,1,2,0:T(2,128)(2,1)} %copy.74), calls=%async_computation.4 | async-start | bytes 1441792 | tf_op jit(solution)/shard_map/all_to_all | solution.py:89
  45.1 23.0 %all-to-all-start.2 = ((bf16[8,2,11,2048]{3,1,2,0:T(2,128)(2,1)}), bf16[8,2,11,2048]{3,1,2,0:T(2,128)(2,1)S(1)}, u32[]{:S(2)}, u32[]{:S(2)}) async-start(bf16[8,2,11,2048]{3,1,2,0:T(2,128)(2,1)} %copy.71), calls=%async_computation.2 | async-start | bytes 1441792 | tf_op jit(solution)/shard_map/all_to_all | solution.py:96
  68.2 12.8 %all-to-all-start.5 = ((bf16[8,2,11,2048]{3,0,2,1:T(8,128)(2,1)}), bf16[8,2,11,2048]{3,0,2,1:T(8,128)(2,1)S(1)}, u32[]{:S(2)}, u32[]{:S(2)}) async-start(bf16[8,2,11,2048]{3,0,2,1:T(8,128)(2,1)} %copy.75), calls=%async_computation.5 | async-start | bytes 1441792 | tf_op jit(solution)/shard_map/all_to_all | solution.py:88
  81.0 11.9 %all-to-all-start.3 = ((bf16[8,2,11,2048]{3,0,2,1:T(8,128)(2,1)}), bf16[8,2,11,2048]{3,0,2,1:T(8,128)(2,1)S(1)}, u32[]{:S(2)}, u32[]{:S(2)}) async-start(bf16[8,2,11,2048]{3,0,2,1:T(8,128)(2,1)} %copy.72), calls=%async_computation.3 | async-start | bytes 1441792 | tf_op jit(solution)/shard_map/all_to_all | solution.py:95
  85.2 3.5 %copy-start = (bf16[2048,1024]{1,0:T(8,128)(2,1)S(1)}, bf16[2048,1024]{1,0:T(8,128)(2,1)}, u32[]{:S(2)}) copy-start(bf16[2048,1024]{1,0:T(8,128)(2,1)} %param.12) | copy-start | bytes 12582916
  99.4 14.7 %all-to-all-start.8 = ((bf16[8,2,11]{2,1,0:T(2,128)(2,1)}), bf16[8,2,11]{2,1,0:T(2,128)(2,1)S(1)}, u32[]{:S(2)}, u32[]{:S(2)}) async-start(bf16[8,2,11]{2,1,0:T(2,128)(2,1)} %convert_element_type.97), calls=%async_computation.8 | async-start | bytes 8192 | tf_op jit(solution)/shard_map/all_to_all | solution.py:133
  112.1 7.2 %copy-start.4 = (s32[24,6]{0,1:T(8,128)S(1)}, s32[24,6]{0,1:T(8,128)}, u32[]{:S(2)}) copy-start(s32[24,6]{0,1:T(8,128)} %param.9) | copy-start | bytes 1732
  114.0 23.8 %all-to-all-start.6 = ((bf16[8,2,11,2048]{3,1,2,0:T(2,128)(2,1)}), bf16[8,2,11,2048]{3,1,2,0:T(2,128)(2,1)S(1)}, u32[]{:S(2)}, u32[]{:S(2)}) async-start(bf16[8,2,11,2048]{3,1,2,0:T(2,128)(2,1)} %copy.77), calls=%async_computation.6 | async-start | bytes 1441792 | tf_op jit(solution)/shard_map/all_to_all | solution.py:120
  119.4 21.6 %copy-start.2 = (bf16[176,1024]{1,0:T(8,128)(2,1)S(1)}, bf16[176,1024]{1,0:T(8,128)(2,1)}, u32[]{:S(2)}) copy-start(bf16[176,1024]{1,0:T(8,128)(2,1)} %get-tuple-element.7) | copy-start | bytes 1081348
  137.8 9.1 %all-to-all-start.9 = ((bf16[8,2,11]{2,0,1:T(8,128)(2,1)}), bf16[8,2,11]{2,0,1:T(8,128)(2,1)S(1)}, u32[]{:S(2)}, u32[]{:S(2)}) async-start(bf16[8,2,11]{2,0,1:T(8,128)(2,1)} %copy.80), calls=%async_computation.9 | async-start | bytes 8192 | tf_op jit(solution)/shard_map/all_to_all | solution.py:132
  141.1 9.3 %copy-start.1 = (bf16[176,1024]{1,0:T(8,128)(2,1)S(1)}, bf16[176,1024]{1,0:T(8,128)(2,1)}, u32[]{:S(2)}) copy-start(bf16[176,1024]{1,0:T(8,128)(2,1)} %get-tuple-element.8) | copy-start | bytes 1081348
  146.9 12.8 %all-to-all-start.7 = ((bf16[8,2,11,2048]{3,0,2,1:T(8,128)(2,1)}), bf16[8,2,11,2048]{3,0,2,1:T(8,128)(2,1)S(1)}, u32[]{:S(2)}, u32[]{:S(2)}) async-start(bf16[8,2,11,2048]{3,0,2,1:T(8,128)(2,1)} %copy.78), calls=%async_computation.7 | async-start | bytes 1441792 | tf_op jit(solution)/shard_map/all_to_all | solution.py:119
where the time goes:
time: 164 us; the launch traced here: 161 us
  waiting for transfers between devices  63.3 us (39%)
  starting transfers between devices  44.2 us (27%)
  matrix products  34.6 us (21%)
  local copies, waits for them, and re-layouts  18.2 us (11%)
    all_to_all x1, waiting for transfers between devices, local(): lax.all_to_all(spread(cotan_slots), 'expert', split_axis=0, concat_axis=0...  17.6 us
    all_to_all x1, waiting for transfers between devices, local(): lax.all_to_all(spread(token_slots), 'expert', split_axis=0, concat_axis=0...  16 us
    all_to_all x1, waiting for transfers between devices, local(): lax.all_to_all(token_partial.reshape(columns, dp_size, slot_most, feature...  12 us
    all_to_all x1, waiting for transfers between devices, local(): lax.all_to_all(lax.all_to_all(spread(token_slots), 'expert', split_axis=0...  8.05 us
    dot_general x1, matrix products, expert_backward(): lax.dot_general(joined_grad, joined_weight, contract_last, preferred_elem...  6.61 us
    all_to_all x1, starting transfers between devices, local(): lax.all_to_all(spread(mix_slots), 'expert', split_axis=0, concat_axis=0,...  6.38 us
    all_to_all x1, starting transfers between devices, local(): lax.all_to_all(mix_partial.reshape(columns, dp_size, slot_most), 'expert'...  6.12 us
    dot_general x1, matrix products, expert_backward(): lax.dot_general(hidden, scaled_cotan, contract_first, preferred_element_t...  5.78 us
  transfers between devices with their start and end apart: 10, of which 8 were waited for; matrix products, arithmetic and copies ran while one was open for 25% of the time, Pallas kernels for 0%

commit v1 on v0

--- a/solution.py
+++ b/solution.py
@@ -40,7 +40,7 @@
     return (token_partial, mix_partial, gate_grad, up_grad, down_grad)
 
 
-def local(tokens, cotangent, routes, mix_weights, gate_matrix, up_matrix, down_matrix):
+def local_exchange(tokens, cotangent, routes, mix_weights, gate_matrix, up_matrix, down_matrix):
     tok_count, features = tokens.shape
     top_count = routes.shape[1]
     columns = lax.axis_size("expert")
@@ -167,7 +167,56 @@
     return (grad_tokens, grad_mix, gate_grad, up_grad, down_grad)
 
 
+def local_gather(tokens, cotangent, routes, mix_weights, gate_matrix, up_matrix, down_matrix):
+    axes = ("expert", "dp")
+    f32, bf16 = jnp.float32, jnp.bfloat16
+    tok_count, features = tokens.shape
+    top_count = routes.shape[1]
+    devices = lax.axis_size("expert") * lax.axis_size("dp")
+    experts = devices
+    slot_most = min(5 * tok_count * top_count // (4 * experts), tok_count)
+    rows = devices * slot_most
+    mine = lax.axis_index("expert") * lax.axis_size("dp") + lax.axis_index("dp")
+    extra = jnp.zeros((tok_count, 128 - 2 * top_count), bf16)
+    packed = jnp.concatenate(
+        [tokens, cotangent, routes.astype(bf16), mix_weights, extra], axis=1
+    )
+    world = lax.all_gather(packed, axes, axis=0, tiled=True)
+    total = devices * tok_count
+    tail = 2 * features
+    named = world[:, tail : tail + top_count] == mine.astype(bf16)
+    weight = jnp.sum(
+        jnp.where(named, world[:, tail + top_count : tail + 2 * top_count], 0).astype(f32), axis=1
+    )
+    hit = jnp.any(named, axis=1).reshape(devices, tok_count)
+    ahead = (
+        jnp.arange(tok_count)[:, None] < jnp.arange(tok_count)[None, :]
+    ).astype(bf16)
+    place = jnp.dot(hit.astype(bf16), ahead, preferred_element_type=f32).astype(jnp.int32)
+    place = place + jnp.arange(devices, dtype=jnp.int32)[:, None] * slot_most
+    place = jnp.where(hit, place, -1).reshape(total)
+    pick = (jnp.arange(rows, dtype=jnp.int32)[:, None] == place[None, :]).astype(bf16)
+    row_both = jnp.dot(pick, world[:, :tail], preferred_element_type=f32).astype(bf16)
+    row_mix = jnp.sum(pick.astype(f32) * weight[None, :], axis=1).astype(bf16)
+    token_partial, mix_partial, gate_grad, up_grad, down_grad = expert_backward(
+        row_both[:, :features], row_both[:, features:], row_mix, gate_matrix, up_matrix, down_matrix
+    )
+    lane = (jnp.arange(128, dtype=jnp.int32)[None, :] == mine).astype(bf16)
+    back = jnp.concatenate([token_partial, mix_partial[:, None] * lane], axis=1)
+    spread = lax.dot_general(
+        pick, back, (((0,), (0,)), ((), ())), preferred_element_type=f32
+    ).astype(bf16)
+    home = lax.psum_scatter(spread, axes, scatter_dimension=0, tiled=True)
+    grad_tokens = home[:, :features]
+    chosen = routes[:, :, None] == jnp.arange(experts, dtype=jnp.int32)[None, None, :]
+    grad_mix = jnp.sum(
+        jnp.where(chosen, home[:, None, features : features + experts].astype(f32), 0.0), axis=2
+    )
+    return (grad_tokens, grad_mix, gate_grad, up_grad, down_grad)
+
+
 def solution(mesh):
+    local = local_gather if mesh.shape["dp"] == 2 else local_exchange
     in_specs = (
         P(("groups", "expert", "dp"), None),
         P(("groups", "expert", "dp"), None),

time: 164 us -> 186 us (1.13)
  waiting for transfers between devices: 63.3 us -> 131 us
  starting transfers between devices: 44.2 us -> 0.08 us
  between operations: 0.91 us -> 14.8 us
  local copies, waits for them, and re-layouts: 18.2 us -> 8.93 us
  matrix products: 34.6 us -> 25.7 us
  other arithmetic: 0.13 us -> 3.88 us
    unnamed x0 -> x3, waiting for transfers between devices: none -> 84.3 us
    all_to_all x10 -> x0, waiting for transfers between devices: 63.3 us -> none  [the longest x1 17.6 us: local(): lax.all_to_all(spread(cotan_slots), 'expert', split_axis=0, concat_axis=0...]
    all_gather x0 -> x1, waiting for transfers between devices: none -> 46.5 us  [local_gather(): world = lax.all_gather(packed, axes, axis=0, tiled=True)]
    all_to_all x10 -> x0, starting transfers between devices: 44.2 us -> none  [the longest x1 6.38 us: local(): lax.all_to_all(spread(mix_slots), 'expert', split_axis=0, concat_axis=0,...]
    all_to_all x9 -> x0, local copies, waits for them, and re-layouts: 5.77 us -> none  [the longest x1 1.11 us: local(): lax.all_to_all(token_partial.reshape(columns, dp_size, slot_most, feature...]
    another operation x7 -> x0, local copies, waits for them, and re-layouts: 4.7 us -> none  [the longest x5 4.5 us: spread(): return wide.reshape((columns, dp_size, slot_most) + rest)]
    dot_general x1, matrix products: 6.61 us -> 2.94 us  [expert_backward(): lax.dot_general(joined_grad, joined_weight, contract_last, preferred_elem...]
    dot_general x1, matrix products: 5.14 us -> 1.91 us  [expert_backward(): lax.dot_general(row_cotan, down_matrix, contract_last, preferred_element_...]
  transfers between devices with their start and end apart: 10 -> 2, of which waited for: 8 -> 2; matrix products, arithmetic and copies ran while one was open for 25% -> 6% of each run, Pallas kernels for 0% -> 0%
where the time goes in v1:
time: 186 us; the launch traced here: 184 us
  waiting for transfers between devices  131 us (70%)
  matrix products  25.7 us (14%)
  between operations  14.8 us (8%)
  local copies, waits for them, and re-layouts  8.93 us (5%)
  other arithmetic  3.88 us (2%)
    unnamed x3, waiting for transfers between devices  84.3 us
    all_gather x1, waiting for transfers between devices, local_gather(): world = lax.all_gather(packed, axes, axis=0, tiled=True)  46.5 us
    dot_general x1, matrix products, expert_backward(): lax.dot_general(hidden, scaled_cotan, contract_first, preferred_element_t...  4.75 us
    dot_general x1, matrix products, expert_backward(): lax.dot_general(row_tokens, grad_pregate, contract_first, preferred_eleme...  4.7 us
    dot_general x1, matrix products, expert_backward(): lax.dot_general(row_tokens, grad_upper, contract_first, preferred_element...  4.69 us
    unnamed x11, local copies, waits for them, and re-layouts  4.57 us
  transfers between devices with their start and end apart: 2, of which 2 were waited for; matrix products, arithmetic and copies ran while one was open for 6% of the time, Pallas kernels for 0%

profile of v1, /device:TPU:1, one launch (start us, length us, event | category | flops | bytes accessed | tf_op | source)
XLA Modules:
  0.0 184.2 jit_solution(17356240670144272698)
XLA Ops:
  7.2 0.7 convert_element_type.82
  8.0 0.8 copy.22
  8.8 1.7 concatenate.12
  10.6 1.2 dynamic-slice
  12.5 46.5 %all-gather.2.cloned.1.call-done = bf16[384,4224]{1,0:T(8,128)(2,1)} async-done(((bf16[24,4224]{1,0:T(8,128)(2,1)}), bf16[384,4224]{1,0:T(8,128)(2,1)}) %all-gather.2.cloned.1.call-update) | async-done | bytes 3244048 | tf_op jit(solution)/shard_map/all_gather | solution.py:184
  59.0 1.0 fusion.33
  60.2 0.2 eq.48
  60.4 1.3 convert_reduce_fusion
  61.6 0.1 multiply_reduce_fusion.1
  61.8 2.8 %convolution_convert_fusion = bf16[176,4096]{1,0:T(8,128)(2,1)S(1)} fusion(bf16[384,4224]{1,0:T(8,128)(2,1)} %all-gather.2.cloned.1.call-done, s32[384]{0:T(512)S(1)} %eq.48), kind=kOutput, calls=%fused_computation.4 | convolution fusion | flops 554436608 | bytes 4589056 | tf_op jit(solution)/shard_map/dot_general | solution.py:199
  64.6 0.9 fusion.26
  65.6 1.2 copy-done
  66.8 0.9 fusion.28
  67.8 1.2 copy-done.3
  69.0 1.9 %multiply_reduce_fusion = (bf16[176]{0:T(256)(128)(2,1)S(1)}, bf16[176,1024]{1,0:T(8,128)(2,1)S(1)}, bf16[176,1024]{1,0:T(8,128)(2,1)S(1)}, bf16[176,1024]{1,0:T(8,128)(2,1)S(1)}) fusion(f32[176,1024]{1,0:T(8,128)S(1)} %fusion.28, f32[176,1024]{1,0:T(8,128)S(1)} %fusion.26, f32[176]{0:T(256)S(1)} %convert_element_type.126, ...), kind=kOutput, calls=%fused_computation.20 | convolution fusion | flops 741621568 | bytes 7439712 | tf_op jit(solution)/shard_map/dot_general | solution.py:15
  70.9 4.7 %fusion.24 = f32[2048,1024]{1,0:T(8,128)} fusion(bf16[176,1024]{1,0:T(8,128)(2,1)S(1)} %get-tuple-element.7, bf16[176,4096]{1,0:T(8,128)(2,1)S(1)} %convolution_convert_fusion), kind=kOutput, calls=%fused_computation.31 | convolution fusion | flops 738197504 | bytes 9469952 | tf_op jit(solution)/shard_map/dot_general | solution.py:29
  75.6 2.9 %fusion.5 = bf16[176,2048]{1,0:T(8,128)(2,1)S(1)} fusion(bf16[2048,1024]{1,0:T(8,128)(2,1)S(1)} %copy-done, bf16[2048,1024]{1,0:T(8,128)(2,1)S(1)} %copy-done.1, bf16[176,1024]{1,0:T(8,128)(2,1)S(1)} %get-tuple-element.8, bf16[176,1024]{1,0:T(8,128)(2,1)S(1)} %get-tuple-element.7), kind=kOutput, calls=%fused_computation.7 | convolution fusion | flops 1494974464 | bytes 9830400 | tf_op jit(solution)/shard_map/dot_general | solution.py:37
  78.7 1.9 %convolution_convert_fusion.1 = bf16[384,2176]{1,0:T(8,128)(2,1)} fusion(bf16[176,128]{1,0:T(8,128)(2,1)S(1)} %broadcast_multiply_fusion, bf16[176,2048]{1,0:T(8,128)(2,1)S(1)} %fusion.5, s32[384]{0:T(512)S(1)} %eq.48), kind=kOutput, calls=%fused_computation.5 | convolution fusion | flops 296560640 | bytes 2438656 | tf_op jit(solution)/shard_map/dot_general | solution.py:206
  80.6 4.7 %fusion.22 = f32[2048,1024]{1,0:T(8,128)} fusion(bf16[176,1024]{1,0:T(8,128)(2,1)S(1)} %get-tuple-element.8, bf16[176,4096]{1,0:T(8,128)(2,1)S(1)} %convolution_convert_fusion), kind=kOutput, calls=%fused_computation.29 | convolution fusion | flops 738197504 | bytes 9469952 | tf_op jit(solution)/shard_map/dot_general | solution.py:32
  85.3 4.8 %fusion.13 = f32[1024,2048]{1,0:T(8,128)} fusion(bf16[176,1024]{1,0:T(8,128)(2,1)S(1)} %get-tuple-element.6, f32[176]{0:T(256)S(1)} %convert_element_type.126, bf16[176,4096]{1,0:T(8,128)(2,1)S(1)} %convolution_convert_fusion), kind=kOutput, calls=%fused_computation.15 | convolution fusion | flops 739278848 | bytes 9470976 | tf_op jit(solution)/shard_map/dot_general | solution.py:26
  90.0 84.3 %all-reduce.3.cloned.1.call-done = bf16[384,2176]{1,0:T(8,128)(2,1)} async-done(((bf16[384,2176]{1,0:T(8,128)(2,1)}), bf16[384,2176]{1,0:T(8,128)(2,1)}) %all-reduce.3.cloned.1.call-update) | async-done | bytes 1671184
  174.3 0.8 dynamic-slice.3
  175.2 0.6 select_reduce_fusion
  175.8 1.5 constant_dynamic-slice_fusion
  (20 shorter events, 0.6 us)
Async XLA Ops:
  7.2 51.8 %all-gather.2.cloned.1.call-start = ((), (), s32[]{:S(2)}) async-start(), calls=%async_computation | async-start | bytes 3446784 | tf_op jit(solution)/shard_map/all_gather | solution.py:184
  10.5 163.8 %all-reduce.3.cloned.1.call-start = ((), (), s32[]{:S(2)}) async-start(), calls=%async_computation.1 | async-start | bytes 3342336
  60.3 4.3 %copy-start.1 = (bf16[2048,1024]{1,0:T(8,128)(2,1)S(1)}, bf16[2048,1024]{1,0:T(8,128)(2,1)}, u32[]{:S(2)}) copy-start(bf16[2048,1024]{1,0:T(8,128)(2,1)} %param.11) | copy-start | bytes 12582916
  64.6 2.2 %copy-start = (bf16[2048,1024]{1,0:T(8,128)(2,1)S(1)}, bf16[2048,1024]{1,0:T(8,128)(2,1)}, u32[]{:S(2)}) copy-start(bf16[2048,1024]{1,0:T(8,128)(2,1)} %param.12) | copy-start | bytes 12582916
  66.8 2.2 %copy-start.3 = (bf16[1024,2048]{1,0:T(8,128)(2,1)S(1)}, bf16[1024,2048]{1,0:T(8,128)(2,1)}, u32[]{:S(2)}) copy-start(bf16[1024,2048]{1,0:T(8,128)(2,1)} %param.13) | copy-start | bytes 12582916
  85.3 89.9 %copy-start.2 = (s32[24,6]{0,1:T(8,128)S(1)}, s32[24,6]{0,1:T(8,128)}, u32[]{:S(2)}) copy-start(s32[24,6]{0,1:T(8,128)} %param.9) | copy-start | bytes 1732
Sparse Core Ops, SparseCore 0:
  10.8 48.1 all-gather.1
  80.7 93.5 all-reduce.2

commit v2 on v1

--- a/solution.py
+++ b/solution.py
@@ -1,6 +1,8 @@
 import jax
 import jax.numpy as jnp
 from jax import lax
+from jax.experimental import pallas as pl
+from jax.experimental.pallas import tpu as pltpu
 from jax.sharding import PartitionSpec as P
 
 
@@ -167,50 +169,326 @@
     return (grad_tokens, grad_mix, gate_grad, up_grad, down_grad)
 
 
+def position():
+    expert = lax.axis_index("expert")
+    return lax.div(expert, 2), lax.rem(expert, 2), lax.axis_index("dp")
+
+
+def device(z, core, x):
+    return {"expert": z * 2 + core, "dp": x}
+
+
+def greet(height, z, core, x):
+    barrier = pltpu.get_barrier_semaphore()
+    above, below = z < height - 1, z > 0
+
+    def signal(target):
+        pl.semaphore_signal(barrier, inc=1, device_id=target, device_id_type=pl.DeviceIdType.MESH)
+
+    signal(device(z, 1 - core, x))
+    signal(device(z, core, 1 - x))
+
+    @pl.when(above)
+    def _():
+        signal(device(z + 1, core, x))
+
+    @pl.when(below)
+    def _():
+        signal(device(z - 1, core, x))
+
+    pl.semaphore_wait(barrier, 2 + above.astype(jnp.int32) + below.astype(jnp.int32))
+
+
+def gather_kernel(height, own_ref, world_ref, send_sem, recv_sem, own_sem):
+    z, core, x = position()
+    greet(height, z, core, x)
+    mine = (z * 2 + core) * 2 + x
+    keep = pltpu.make_async_copy(own_ref, world_ref.at[mine], own_sem)
+    keep.start()
+    near = [0]
+    for step in range(1, height):
+        near += [-step, step]
+
+    def each(act):
+        for shift in near:
+            for other in (0, 1):
+                from_z = z + shift
+                from_x = x if other == 0 else 1 - x
+
+                @pl.when((from_z >= 0) & (from_z < height))
+                def _():
+                    slot = (from_z * 2 + core) * 2 + from_x
+                    local = shift == 0 and other == 0
+                    source = own_ref if local else world_ref.at[slot]
+
+                    def copy(kind, target):
+                        return pltpu.make_async_remote_copy(
+                            src_ref=source,
+                            dst_ref=world_ref.at[slot],
+                            send_sem=send_sem.at[kind, slot],
+                            recv_sem=recv_sem.at[slot],
+                            device_id=target,
+                            device_id_type=pl.DeviceIdType.MESH,
+                        )
+
+                    along = (core == 0) | (other == 0)
+                    act(local, slot, [
+                        (along & (z < height - 1) if shift <= 0 else None,
+                         lambda: copy(0, device(z + 1, core, x))),
+                        (along & (z > 0) if shift >= 0 else None,
+                         lambda: copy(1, device(z - 1, core, x))),
+                        ((core == 1) | (shift == 0) if other == 0 else None,
+                         lambda: copy(2, device(z, core, 1 - x))),
+                        (True, lambda: copy(3, device(z, 1 - core, x))),
+                    ])
+
+    def arrive(slot):
+        pltpu.make_async_remote_copy(
+            src_ref=world_ref.at[slot],
+            dst_ref=world_ref.at[slot],
+            send_sem=send_sem.at[0, slot],
+            recv_sem=recv_sem.at[slot],
+            device_id=device(z, 1 - core, x),
+            device_id_type=pl.DeviceIdType.MESH,
+        ).wait_recv()
+
+    def forward(local, slot, moves):
+        if not local:
+            arrive(slot)
+        for when, make in moves:
+            if when is None:
+                continue
+            if when is True:
+                make().start()
+            else:
+                @pl.when(when)
+                def _():
+                    make().start()
+
+    def settle(local, slot, moves):
+        for when, make in moves:
+            if when is None:
+                continue
+            if when is True:
+                make().wait_send()
+            else:
+                @pl.when(when)
+                def _():
+                    make().wait_send()
+
+    each(forward)
+    for from_z in range(height):
+        for from_x in range(2):
+            arrive((from_z * 2 + 1 - core) * 2 + from_x)
+    each(settle)
+    keep.wait()
+
+
+def gather(own, height):
+    slots = 4 * height
+    vmem = pl.BlockSpec(memory_space=pltpu.VMEM)
+    return pl.pallas_call(
+        lambda *refs: gather_kernel(height, *refs),
+        out_shape=jax.ShapeDtypeStruct((slots,) + own.shape, own.dtype),
+        in_specs=[vmem],
+        out_specs=vmem,
+        scratch_shapes=[
+            pltpu.SemaphoreType.DMA((4, slots)),
+            pltpu.SemaphoreType.DMA((slots,)),
+            pltpu.SemaphoreType.DMA,
+        ],
+        compiler_params=pltpu.CompilerParams(
+            collective_id=0, has_side_effects=True, vmem_limit_bytes=24 * 1024 * 1024
+        ),
+    )(own)
+
+
+def reduce_kernel(height, own_ref, out_ref, core_in, up_in, down_in, x_in, staged, total,
+                  core_send, core_recv, flow_send, up_recv, down_recv, x_recv):
+    z, core, x = position()
+    greet(height, z, core, x)
+    f32 = jnp.float32
+
+    def move(source, target_ref, send, recv, target):
+        return pltpu.make_async_remote_copy(
+            src_ref=source, dst_ref=target_ref, send_sem=send, recv_sem=recv,
+            device_id=target, device_id_type=pl.DeviceIdType.MESH,
+        )
+
+    far = []
+    for step in range(height - 1, 0, -1):
+        far += [step, -step]
+    far += [0]
+
+    def each(act):
+        for shift in far:
+            for other in (1, 0):
+                to_z = z + shift
+                to_x = x if other == 0 else 1 - x
+
+                @pl.when((to_z >= 0) & (to_z < height))
+                def _():
+                    act(shift, other, to_z, to_x, to_z * 2 + to_x)
+
+    def over_core(to_z, to_x, block):
+        return move(
+            own_ref.at[(to_z * 2 + 1 - core) * 2 + to_x], core_in.at[block],
+            core_send.at[block], core_recv.at[block], device(z, 1 - core, x),
+        )
+
+    def over_x(to_z, block):
+        return move(
+            staged.at[block], x_in.at[to_z], flow_send.at[block], x_recv.at[to_z],
+            device(z, core, 1 - x),
+        )
+
+    def over_up(block):
+        return move(
+            staged.at[block], up_in.at[block], flow_send.at[block], up_recv.at[block],
+            device(z + 1, core, x),
+        )
+
+    def over_down(block):
+        return move(
+            staged.at[block], down_in.at[block], flow_send.at[block], down_recv.at[block],
+            device(z - 1, core, x),
+        )
+
+    def add(ref):
+        total[...] += ref[...].astype(f32)
+
+    def launch(shift, other, to_z, to_x, block):
+        over_core(to_z, to_x, block).start()
+
+    def work(shift, other, to_z, to_x, block):
+        over_core(to_z, to_x, block).wait_recv()
+        total[...] = own_ref[(to_z * 2 + core) * 2 + to_x].astype(f32) + core_in[block].astype(f32)
+        along = True if other == 0 else core == 0
+        if other == 0:
+            @pl.when((core == 1) | (shift == 0))
+            def _():
+                over_x(to_z, block).wait_recv()
+                add(x_in.at[to_z])
+        if shift >= 0:
+            @pl.when(along & (z > 0))
+            def _():
+                over_up(block).wait_recv()
+                add(up_in.at[block])
+        if shift <= 0:
+            @pl.when(along & (z < height - 1))
+            def _():
+                over_down(block).wait_recv()
+                add(down_in.at[block])
+        if shift == 0 and other == 0:
+            out_ref[...] = total[...].astype(out_ref.dtype)
+        else:
+            staged[block] = total[...].astype(staged.dtype)
+            flow(shift, other, to_z, block, lambda copy: copy.start())
+
+    def flow(shift, other, to_z, block, act):
+        if other == 1 and shift == 0:
+            act(over_x(to_z, block))
+            return
+        passing = over_up if shift > 0 else over_down
+        if other == 0:
+            act(passing(block))
+            return
+
+        @pl.when(core == 0)
+        def _():
+            act(passing(block))
+
+        @pl.when(core == 1)
+        def _():
+            act(over_x(to_z, block))
+
+    def settle(shift, other, to_z, to_x, block):
+        over_core(to_z, to_x, block).wait_send()
+        if not (shift == 0 and other == 0):
+            flow(shift, other, to_z, block, lambda copy: copy.wait_send())
+
+    each(launch)
+    each(work)
+    each(settle)
+
+
+def scatter_sum(parts, height):
+    vmem = pl.BlockSpec(memory_space=pltpu.VMEM)
+    block = parts.shape[1:]
+    dma = pltpu.SemaphoreType.DMA
+    half = 2 * height
+    return pl.pallas_call(
+        lambda *refs: reduce_kernel(height, *refs),
+        out_shape=jax.ShapeDtypeStruct(block, parts.dtype),
+        in_specs=[vmem],
+        out_specs=vmem,
+        scratch_shapes=[
+            pltpu.VMEM((half,) + block, parts.dtype),
+            pltpu.VMEM((half,) + block, parts.dtype),
+            pltpu.VMEM((half,) + block, parts.dtype),
+            pltpu.VMEM((height,) + block, parts.dtype),
+            pltpu.VMEM((half,) + block, parts.dtype),
+            pltpu.VMEM(block, jnp.float32),
+            dma((half,)), dma((half,)), dma((half,)), dma((half,)), dma((half,)), dma((height,)),
+        ],
+        compiler_params=pltpu.CompilerParams(
+            collective_id=1, has_side_effects=True, vmem_limit_bytes=24 * 1024 * 1024
+        ),
+    )(parts)
+
+
 def local_gather(tokens, cotangent, routes, mix_weights, gate_matrix, up_matrix, down_matrix):
-    axes = ("expert", "dp")
     f32, bf16 = jnp.float32, jnp.bfloat16
     tok_count, features = tokens.shape
     top_count = routes.shape[1]
-    devices = lax.axis_size("expert") * lax.axis_size("dp")
-    experts = devices
+    height = lax.axis_size("expert") // 2
+    devices = experts = lax.axis_size("expert") * lax.axis_size("dp")
     slot_most = min(5 * tok_count * top_count // (4 * experts), tok_count)
     rows = devices * slot_most
     mine = lax.axis_index("expert") * lax.axis_size("dp") + lax.axis_index("dp")
-    extra = jnp.zeros((tok_count, 128 - 2 * top_count), bf16)
+    named = jnp.concatenate([routes.astype(bf16), mix_weights], axis=1)
+    named = jnp.pad(named, ((0, tok_count), (0, 128 - 2 * top_count)))
     packed = jnp.concatenate(
-        [tokens, cotangent, routes.astype(bf16), mix_weights, extra], axis=1
-    )
-    world = lax.all_gather(packed, axes, axis=0, tiled=True)
-    total = devices * tok_count
-    tail = 2 * features
-    named = world[:, tail : tail + top_count] == mine.astype(bf16)
-    weight = jnp.sum(
-        jnp.where(named, world[:, tail + top_count : tail + 2 * top_count], 0).astype(f32), axis=1
-    )
-    hit = jnp.any(named, axis=1).reshape(devices, tok_count)
+        [jnp.concatenate([tokens, cotangent], axis=0), named], axis=1
+    )
+    world = gather(packed, height)
+    named = world[:, :tok_count, features : features + top_count] == mine.astype(bf16)
+    heavy = world[:, :tok_count, features + top_count : features + 2 * top_count]
+    weight = jnp.sum(jnp.where(named, heavy, 0).astype(f32), axis=2)
+    hit = jnp.any(named, axis=2)
     ahead = (
         jnp.arange(tok_count)[:, None] < jnp.arange(tok_count)[None, :]
     ).astype(bf16)
     place = jnp.dot(hit.astype(bf16), ahead, preferred_element_type=f32).astype(jnp.int32)
     place = place + jnp.arange(devices, dtype=jnp.int32)[:, None] * slot_most
-    place = jnp.where(hit, place, -1).reshape(total)
-    pick = (jnp.arange(rows, dtype=jnp.int32)[:, None] == place[None, :]).astype(bf16)
-    row_both = jnp.dot(pick, world[:, :tail], preferred_element_type=f32).astype(bf16)
-    row_mix = jnp.sum(pick.astype(f32) * weight[None, :], axis=1).astype(bf16)
+    place = jnp.where(hit, place, -1)
+    place_both = jnp.concatenate([place, jnp.where(hit, place + rows, -1)], axis=1)
+    place_both = place_both.reshape(devices * 2 * tok_count)
+    pick = (jnp.arange(2 * rows, dtype=jnp.int32)[:, None] == place_both[None, :]).astype(bf16)
+    flat = world.reshape(devices * 2 * tok_count, world.shape[2])[:, :features]
+    row_both = jnp.dot(pick, flat, preferred_element_type=f32).astype(bf16)
+    weight_both = jnp.pad(weight, ((0, 0), (0, tok_count))).reshape(-1)
+    row_mix = jnp.sum(pick[:rows].astype(f32) * weight_both[None, :], axis=1).astype(bf16)
     token_partial, mix_partial, gate_grad, up_grad, down_grad = expert_backward(
-        row_both[:, :features], row_both[:, features:], row_mix, gate_matrix, up_matrix, down_matrix
+        row_both[:rows], row_both[rows:], row_mix, gate_matrix, up_matrix, down_matrix
     )
     lane = (jnp.arange(128, dtype=jnp.int32)[None, :] == mine).astype(bf16)
-    back = jnp.concatenate([token_partial, mix_partial[:, None] * lane], axis=1)
+    half = features // 2
+    back = jnp.concatenate(
+        [
+            jnp.concatenate([token_partial[:, :half], token_partial[:, half:]], axis=0),
+            jnp.pad(mix_partial[:, None] * lane, ((0, rows), (0, 0))),
+        ],
+        axis=1,
+    )
     spread = lax.dot_general(
         pick, back, (((0,), (0,)), ((), ())), preferred_element_type=f32
     ).astype(bf16)
-    home = lax.psum_scatter(spread, axes, scatter_dimension=0, tiled=True)
-    grad_tokens = home[:, :features]
+    home = scatter_sum(spread.reshape(devices, 2 * tok_count, half + 128), height)
+    grad_tokens = jnp.concatenate([home[:tok_count, :half], home[tok_count:, :half]], axis=1)
     chosen = routes[:, :, None] == jnp.arange(experts, dtype=jnp.int32)[None, None, :]
     grad_mix = jnp.sum(
-        jnp.where(chosen, home[:, None, features : features + experts].astype(f32), 0.0), axis=2
+        jnp.where(chosen, home[:tok_count, None, half : half + experts].astype(f32), 0.0), axis=2
     )
     return (grad_tokens, grad_mix, gate_grad, up_grad, down_grad)
 

time: 186 us -> 83.5 us (0.45)
  waiting for transfers between devices: 131 us -> 0 us
  Pallas kernels: 0 us -> 49.9 us
  between operations: 14.8 us -> 0.82 us
  local copies, waits for them, and re-layouts: 8.93 us -> 4.05 us
  matrix products: 25.7 us -> 23.5 us
    unnamed x3 -> x0, waiting for transfers between devices: 84.3 us -> none
    pallas_call x0 -> x2, Pallas kernels: none -> 49.9 us  [the longest x1 30.4 us: gather(): pl.pallas_call(lambda *refs: gather_kernel(height, *refs), out_shape=jax....]
    all_gather x1 -> x0, waiting for transfers between devices: 46.5 us -> none  [local_gather(): world = lax.all_gather(packed, axes, axis=0, tiled=True)]
    slice x2, local copies, waits for them, and re-layouts: 2.31 us -> 0.06 us  [the longest x1 0.05 us: local_gather(): token_partial[:, :half]]
    unnamed x11 -> x13, local copies, waits for them, and re-layouts: 4.57 us -> 3.67 us
  transfers between devices with their start and end apart: 2 -> 0, of which waited for: 2 -> 0; matrix products, arithmetic and copies ran while one was open for 6% -> 0% of each run, Pallas kernels for 0% -> 0%
where the time goes in v2:
time: 83.5 us; the launch traced here: 82.3 us
  Pallas kernels  49.9 us (60%)
  matrix products  23.5 us (28%)
  other arithmetic  4.1 us (5%)
  local copies, waits for them, and re-layouts  4.05 us (5%)
    pallas_call x1, Pallas kernels, gather(): pl.pallas_call(lambda *refs: gather_kernel(height, *refs), out_shape=jax....  30.4 us
    pallas_call x1, Pallas kernels, scatter_sum(): pl.pallas_call(lambda *refs: reduce_kernel(height, *refs), out_shape=jax....  19.4 us
    dot_general x1, matrix products, expert_backward(): lax.dot_general(hidden, scaled_cotan, contract_first, preferred_element_t...  4.76 us
    dot_general x1, matrix products, expert_backward(): lax.dot_general(row_tokens, grad_pregate, contract_first, preferred_eleme...  4.69 us
    dot_general x1, matrix products, expert_backward(): lax.dot_general(row_tokens, grad_upper, contract_first, preferred_element...  4.69 us
    unnamed x13, local copies, waits for them, and re-layouts  3.67 us
    dot_general x1, matrix products, expert_backward(): lax.dot_general(joined_grad, joined_weight, contract_last, preferred_elem...  2.97 us
    dot_general x1, matrix products, expert_backward(): lax.dot_general(row_cotan, down_matrix, contract_last, preferred_element_...  1.89 us

profile of v2, /device:TPU:1, one launch (start us, length us, event | category | flops | bytes accessed | tf_op | source)
XLA Modules:
  0.0 82.3 jit_solution(14342260199226760125)
XLA Ops:
  0.7 0.7 convert_element_type.86
  1.5 0.8 copy.19
  2.3 1.0 %pad_maximum_fusion.refs_0_ = bf16[48,2176]{1,0:T(8,128)(2,1)S(1)} fusion(bf16[48,128]{1,0:T(8,128)(2,1)S(1)} %fusion.47, bf16[24,2048]{1,0:T(8,128)(2,1)} %param.8, bf16[24,2048]{1,0:T(8,128)(2,1)} %param.7), kind=kLoop, calls=%fused_computation.49 | loop fusion | flops 626688 | bytes 417792 | tf_op jit(solution)/shard_map/concatenate | solution.py:451
  3.3 30.4 %shard_map.110 = bf16[16,48,2176]{2,1,0:T(8,128)(2,1)S(1)} custom-call(bf16[48,2176]{1,0:T(8,128)(2,1)S(1)} %pad_maximum_fusion.refs_0_), custom_call_target="tpu_custom_call" | custom-call | tf_op jit(solution)/shard_map/pallas_call | solution.py:290
  33.7 0.4 fusion.48
  34.1 0.2 convert_reduce_fusion
  34.4 0.1 pad_add_fusion
  34.7 1.3 %fusion.6 = bf16[352,2048]{1,0:T(8,128)(2,1)S(1)} fusion(bf16[768,2176]{1,0:T(8,128)(2,1)S(1)} %bitcast.9, s32[768]{0:T(1024)S(1)} %eq.48), kind=kOutput, calls=%fused_computation.7 | convolution fusion | flops 1108287488 | bytes 4591616 | tf_op jit(solution)/shard_map/dot_general | solution.py:469
  36.0 0.2 iota_compare_fusion.1
  36.1 0.2 multiply_reduce_fusion.1
  36.3 0.5 copy-done.3
  36.8 0.9 %fusion.37 = f32[176,1024]{1,0:T(8,128)S(1)} fusion(bf16[2048,1024]{1,0:T(8,128)(2,1)S(1)} %copy-done.3, bf16[352,2048]{1,0:T(8,128)(2,1)S(1)} %fusion.6), kind=kOutput, calls=%fused_computation.44 | convolution fusion | flops 738197504 | bytes 5636096 | tf_op jit(solution)/shard_map/dot_general | solution.py:12
  37.8 1.1 %copy-done.2 = bf16[2048,1024]{1,0:T(8,128)(2,1)S(1)} copy-done((bf16[2048,1024]{1,0:T(8,128)(2,1)S(1)}, bf16[2048,1024]{1,0:T(8,128)(2,1)}, u32[]{:S(2)}) %copy-start.2) | copy-done | bytes 4194328
  38.9 0.9 %fusion.39 = f32[176,1024]{1,0:T(8,128)S(1)} fusion(bf16[2048,1024]{1,0:T(8,128)(2,1)S(1)} %copy-done.2, bf16[352,2048]{1,0:T(8,128)(2,1)S(1)} %fusion.6), kind=kOutput, calls=%fused_computation.46 | convolution fusion | flops 738197504 | bytes 5636096 | tf_op jit(solution)/shard_map/dot_general | solution.py:13
  39.9 1.2 %copy-done.5 = bf16[1024,2048]{1,0:T(8,128)(2,1)S(1)} copy-done((bf16[1024,2048]{1,0:T(8,128)(2,1)S(1)}, bf16[1024,2048]{1,0:T(8,128)(2,1)}, u32[]{:S(2)}) %copy-start.5) | copy-done | bytes 4194328
  41.1 1.9 %multiply_reduce_fusion = (bf16[176]{0:T(256)(128)(2,1)S(1)}, bf16[176,1024]{1,0:T(8,128)(2,1)S(1)}, bf16[176,1024]{1,0:T(8,128)(2,1)S(1)}, bf16[176,1024]{1,0:T(8,128)(2,1)S(1)}) fusion(f32[176,1024]{1,0:T(8,128)S(1)} %fusion.39, f32[176,1024]{1,0:T(8,128)S(1)} %fusion.37, f32[176]{0:T(256)S(1)} %convert_element_type.127, ...), kind=kOutput, calls=%fused_computation.27 | convolution fusion | flops 741621568 | bytes 7439712 | tf_op jit(solution)/shard_map/dot_general | solution.py:17
  43.1 3.0 %fusion.9 = bf16[176,2048]{1,0:T(8,128)(2,1)S(1)} fusion(bf16[2048,1024]{1,0:T(8,128)(2,1)S(1)} %copy-done.2, bf16[2048,1024]{1,0:T(8,128)(2,1)S(1)} %copy-done.3, bf16[176,1024]{1,0:T(8,128)(2,1)S(1)} %get-tuple-element.8, bf16[176,1024]{1,0:T(8,128)(2,1)S(1)} %get-tuple-element.7), kind=kOutput, calls=%fused_computation.8 | convolution fusion | flops 1494974464 | bytes 9830400 | tf_op jit(solution)/shard_map/dot_general | solution.py:39
  46.1 1.2 %convolution_convert_fusion = bf16[768,1152]{1,0:T(8,128)(2,1)S(1)} fusion(bf16[176,128]{1,0:T(8,128)(2,1)S(1)} %broadcast_multiply_fusion, bf16[176,1024]{1,0:T(8,128)(2,1)S(1)} %get-tuple-element.10, bf16[176,1024]{1,0:T(8,128)(2,1)S(1)} %get-tuple-element.9, s32[768]{0:T(1024)S(1)} %eq.48), kind=kOutput, calls=%fused_computation.4 | convolution fusion | flops 627253248 | bytes 2538496 | tf_op jit(solution)/shard_map/dot_general | solution.py:484
  47.4 19.4 %shard_map.111 = bf16[48,1152]{1,0:T(8,128)(2,1)S(1)} custom-call(bf16[16,48,1152]{2,1,0:T(8,128)(2,1)S(1)} %bitcast.10), custom_call_target="tpu_custom_call" | custom-call | tf_op jit(solution)/shard_map/pallas_call | solution.py:420
  66.9 0.6 select_reduce_fusion
  67.5 0.6 pad_maximum_fusion.1
  68.2 4.7 %fusion.35 = f32[2048,1024]{1,0:T(8,128)} fusion(bf16[176,1024]{1,0:T(8,128)(2,1)S(1)} %get-tuple-element.7, bf16[352,2048]{1,0:T(8,128)(2,1)S(1)} %copy-done.1), kind=kOutput, calls=%fused_computation.42 | convolution fusion | flops 738197504 | bytes 9469952 | tf_op jit(solution)/shard_map/dot_general | solution.py:31
  72.9 4.7 %fusion.33 = f32[2048,1024]{1,0:T(8,128)} fusion(bf16[176,1024]{1,0:T(8,128)(2,1)S(1)} %get-tuple-element.8, bf16[352,2048]{1,0:T(8,128)(2,1)S(1)} %copy-done.1), kind=kOutput, calls=%fused_computation.40 | convolution fusion | flops 738197504 | bytes 9469952 | tf_op jit(solution)/shard_map/dot_general | solution.py:34
  77.6 4.8 %fusion.22 = f32[1024,2048]{1,0:T(8,128)} fusion(bf16[176,1024]{1,0:T(8,128)(2,1)S(1)} %get-tuple-element.6, f32[176]{0:T(256)S(1)} %convert_element_type.127, bf16[352,2048]{1,0:T(8,128)(2,1)S(1)} %copy-done.1), kind=kOutput, calls=%fused_computation.22 | convolution fusion | flops 739278848 | bytes 9470976 | tf_op jit(solution)/shard_map/dot_general | solution.py:28
  (23 shorter events, 0.7 us)
Async XLA Ops:
  34.6 2.2 %copy-start.3 = (bf16[2048,1024]{1,0:T(8,128)(2,1)S(1)}, bf16[2048,1024]{1,0:T(8,128)(2,1)}, u32[]{:S(2)}) copy-start(bf16[2048,1024]{1,0:T(8,128)(2,1)} %param.11) | copy-start | bytes 12582916
  36.0 3.9 %copy-start = (bf16[352,2048]{1,0:T(8,128)(2,1)}, bf16[352,2048]{1,0:T(8,128)(2,1)S(1)}, u32[]{:S(2)}) copy-start(bf16[352,2048]{1,0:T(8,128)(2,1)S(1)} %fusion.6) | copy-start | bytes 4325380
  36.0 2.9 %copy-start.2 = (bf16[2048,1024]{1,0:T(8,128)(2,1)S(1)}, bf16[2048,1024]{1,0:T(8,128)(2,1)}, u32[]{:S(2)}) copy-start(bf16[2048,1024]{1,0:T(8,128)(2,1)} %param.12) | copy-start | bytes 12582916
  38.9 2.2 %copy-start.5 = (bf16[1024,2048]{1,0:T(8,128)(2,1)S(1)}, bf16[1024,2048]{1,0:T(8,128)(2,1)}, u32[]{:S(2)}) copy-start(bf16[1024,2048]{1,0:T(8,128)(2,1)} %param.13) | copy-start | bytes 12582916
  46.1 20.8 %copy-start.4 = (s32[24,6]{0,1:T(8,128)S(1)}, s32[24,6]{0,1:T(8,128)}, u32[]{:S(2)}) copy-start(s32[24,6]{0,1:T(8,128)} %param.9) | copy-start | bytes 1732
  46.1 22.1 %copy-start.1 = (bf16[352,2048]{1,0:T(8,128)(2,1)S(1)}, bf16[352,2048]{1,0:T(8,128)(2,1)}, u32[]{:S(2)}) copy-start(bf16[352,2048]{1,0:T(8,128)(2,1)} %copy-done) | copy-start | bytes 4325380

commit v3 on v2

--- a/solution.py
+++ b/solution.py
@@ -209,9 +209,12 @@
     for step in range(1, height):
         near += [-step, step]
 
+    cut = own_ref.shape[0] // 48 * 32
+    pieces = (pl.ds(0, cut), pl.ds(cut, own_ref.shape[0] - cut))
+
     def each(act):
         for shift in near:
-            for other in (0, 1):
+            for other, piece in ((0, 0), (0, 1), (1, 0), (1, 1)):
                 from_z = z + shift
                 from_x = x if other == 0 else 1 - x
 
@@ -219,20 +222,21 @@
                 def _():
                     slot = (from_z * 2 + core) * 2 + from_x
                     local = shift == 0 and other == 0
-                    source = own_ref if local else world_ref.at[slot]
+                    part = world_ref.at[slot, pieces[piece]]
+                    source = own_ref.at[pieces[piece]] if local else part
 
                     def copy(kind, target):
                         return pltpu.make_async_remote_copy(
                             src_ref=source,
-                            dst_ref=world_ref.at[slot],
-                            send_sem=send_sem.at[kind, slot],
-                            recv_sem=recv_sem.at[slot],
+                            dst_ref=part,
+                            send_sem=send_sem.at[kind, slot, piece],
+                            recv_sem=recv_sem.at[slot, piece],
                             device_id=target,
                             device_id_type=pl.DeviceIdType.MESH,
                         )
 
                     along = (core == 0) | (other == 0)
-                    act(local, slot, [
+                    act(local, slot, piece, [
                         (along & (z < height - 1) if shift <= 0 else None,
                          lambda: copy(0, device(z + 1, core, x))),
                         (along & (z > 0) if shift >= 0 else None,
@@ -242,19 +246,19 @@
                         (True, lambda: copy(3, device(z, 1 - core, x))),
                     ])
 
-    def arrive(slot):
+    def arrive(slot, piece):
         pltpu.make_async_remote_copy(
-            src_ref=world_ref.at[slot],
-            dst_ref=world_ref.at[slot],
-            send_sem=send_sem.at[0, slot],
-            recv_sem=recv_sem.at[slot],
+            src_ref=world_ref.at[slot, pieces[piece]],
+            dst_ref=world_ref.at[slot, pieces[piece]],
+            send_sem=send_sem.at[0, slot, piece],
+            recv_sem=recv_sem.at[slot, piece],
             device_id=device(z, 1 - core, x),
             device_id_type=pl.DeviceIdType.MESH,
         ).wait_recv()
 
-    def forward(local, slot, moves):
+    def forward(local, slot, piece, moves):
         if not local:
-            arrive(slot)
+            arrive(slot, piece)
         for when, make in moves:
             if when is None:
                 continue
@@ -265,7 +269,7 @@
                 def _():
                     make().start()
 
-    def settle(local, slot, moves):
+    def settle(local, slot, piece, moves):
         for when, make in moves:
             if when is None:
                 continue
@@ -279,7 +283,8 @@
     each(forward)
     for from_z in range(height):
         for from_x in range(2):
-            arrive((from_z * 2 + 1 - core) * 2 + from_x)
+            for piece in range(2):
+                arrive((from_z * 2 + 1 - core) * 2 + from_x, piece)
     each(settle)
     keep.wait()
 
@@ -293,8 +298,8 @@
         in_specs=[vmem],
         out_specs=vmem,
         scratch_shapes=[
-            pltpu.SemaphoreType.DMA((4, slots)),
-            pltpu.SemaphoreType.DMA((slots,)),
+            pltpu.SemaphoreType.DMA((4, slots, 2)),
+            pltpu.SemaphoreType.DMA((slots, 2)),
             pltpu.SemaphoreType.DMA,
         ],
         compiler_params=pltpu.CompilerParams(

time: 83.5 us -> 82.8 us (level); the launches traced: 82.3 us -> 82.5 us
  no operation moved by 1% of the time
where the time goes in v3:
time: 82.8 us; the launch traced here: 82.5 us
  Pallas kernels  50 us (60%)
  matrix products  23.5 us (28%)
  other arithmetic  4.1 us (5%)
  local copies, waits for them, and re-layouts  4.06 us (5%)
    pallas_call x1, Pallas kernels, gather(): pl.pallas_call(lambda *refs: gather_kernel(height, *refs), out_shape=jax....  30.6 us
    pallas_call x1, Pallas kernels, scatter_sum(): pl.pallas_call(lambda *refs: reduce_kernel(height, *refs), out_shape=jax....  19.4 us
    dot_general x1, matrix products, expert_backward(): lax.dot_general(hidden, scaled_cotan, contract_first, preferred_element_t...  4.76 us
    dot_general x1, matrix products, expert_backward(): lax.dot_general(row_tokens, grad_pregate, contract_first, preferred_eleme...  4.69 us
    dot_general x1, matrix products, expert_backward(): lax.dot_general(row_tokens, grad_upper, contract_first, preferred_element...  4.69 us
    unnamed x13, local copies, waits for them, and re-layouts  3.68 us
    dot_general x1, matrix products, expert_backward(): lax.dot_general(joined_grad, joined_weight, contract_last, preferred_elem...  2.97 us
    dot_general x1, matrix products, expert_backward(): lax.dot_general(row_cotan, down_matrix, contract_last, preferred_element_...  1.89 us

profile of v3, /device:TPU:1, one launch (start us, length us, event | category | flops | bytes accessed | tf_op | source)
XLA Modules:
  0.0 82.5 jit_solution(4364539768620898416)
XLA Ops:
  0.7 0.7 convert_element_type.86
  1.5 0.8 copy.19
  2.3 1.0 %pad_maximum_fusion.refs_0_ = bf16[48,2176]{1,0:T(8,128)(2,1)S(1)} fusion(bf16[48,128]{1,0:T(8,128)(2,1)S(1)} %fusion.47, bf16[24,2048]{1,0:T(8,128)(2,1)} %param.8, bf16[24,2048]{1,0:T(8,128)(2,1)} %param.7), kind=kLoop, calls=%fused_computation.49 | loop fusion | flops 626688 | bytes 417792 | tf_op jit(solution)/shard_map/concatenate | solution.py:456
  3.3 30.6 %shard_map.110 = bf16[16,48,2176]{2,1,0:T(8,128)(2,1)S(1)} custom-call(bf16[48,2176]{1,0:T(8,128)(2,1)S(1)} %pad_maximum_fusion.refs_0_), custom_call_target="tpu_custom_call" | custom-call | tf_op jit(solution)/shard_map/pallas_call | solution.py:295
  33.9 0.4 fusion.48
  34.2 0.2 convert_reduce_fusion
  34.6 0.1 pad_add_fusion
  34.8 1.3 %fusion.6 = bf16[352,2048]{1,0:T(8,128)(2,1)S(1)} fusion(bf16[768,2176]{1,0:T(8,128)(2,1)S(1)} %bitcast.9, s32[768]{0:T(1024)S(1)} %eq.48), kind=kOutput, calls=%fused_computation.7 | convolution fusion | flops 1108287488 | bytes 4591616 | tf_op jit(solution)/shard_map/dot_general | solution.py:474
  36.1 0.2 iota_compare_fusion.1
  36.3 0.2 multiply_reduce_fusion.1
  36.5 0.5 copy-done.3
  37.0 0.9 %fusion.37 = f32[176,1024]{1,0:T(8,128)S(1)} fusion(bf16[2048,1024]{1,0:T(8,128)(2,1)S(1)} %copy-done.3, bf16[352,2048]{1,0:T(8,128)(2,1)S(1)} %fusion.6), kind=kOutput, calls=%fused_computation.44 | convolution fusion | flops 738197504 | bytes 5636096 | tf_op jit(solution)/shard_map/dot_general | solution.py:12
  38.0 1.1 %copy-done.2 = bf16[2048,1024]{1,0:T(8,128)(2,1)S(1)} copy-done((bf16[2048,1024]{1,0:T(8,128)(2,1)S(1)}, bf16[2048,1024]{1,0:T(8,128)(2,1)}, u32[]{:S(2)}) %copy-start.2) | copy-done | bytes 4194328
  39.1 0.9 %fusion.39 = f32[176,1024]{1,0:T(8,128)S(1)} fusion(bf16[2048,1024]{1,0:T(8,128)(2,1)S(1)} %copy-done.2, bf16[352,2048]{1,0:T(8,128)(2,1)S(1)} %fusion.6), kind=kOutput, calls=%fused_computation.46 | convolution fusion | flops 738197504 | bytes 5636096 | tf_op jit(solution)/shard_map/dot_general | solution.py:13
  40.0 1.2 %copy-done.5 = bf16[1024,2048]{1,0:T(8,128)(2,1)S(1)} copy-done((bf16[1024,2048]{1,0:T(8,128)(2,1)S(1)}, bf16[1024,2048]{1,0:T(8,128)(2,1)}, u32[]{:S(2)}) %copy-start.5) | copy-done | bytes 4194328
  41.3 1.9 %multiply_reduce_fusion = (bf16[176]{0:T(256)(128)(2,1)S(1)}, bf16[176,1024]{1,0:T(8,128)(2,1)S(1)}, bf16[176,1024]{1,0:T(8,128)(2,1)S(1)}, bf16[176,1024]{1,0:T(8,128)(2,1)S(1)}) fusion(f32[176,1024]{1,0:T(8,128)S(1)} %fusion.39, f32[176,1024]{1,0:T(8,128)S(1)} %fusion.37, f32[176]{0:T(256)S(1)} %convert_element_type.127, ...), kind=kOutput, calls=%fused_computation.27 | convolution fusion | flops 741621568 | bytes 7439712 | tf_op jit(solution)/shard_map/dot_general | solution.py:17
  43.2 3.0 %fusion.9 = bf16[176,2048]{1,0:T(8,128)(2,1)S(1)} fusion(bf16[2048,1024]{1,0:T(8,128)(2,1)S(1)} %copy-done.2, bf16[2048,1024]{1,0:T(8,128)(2,1)S(1)} %copy-done.3, bf16[176,1024]{1,0:T(8,128)(2,1)S(1)} %get-tuple-element.8, bf16[176,1024]{1,0:T(8,128)(2,1)S(1)} %get-tuple-element.7), kind=kOutput, calls=%fused_computation.8 | convolution fusion | flops 1494974464 | bytes 9830400 | tf_op jit(solution)/shard_map/dot_general | solution.py:39
  46.3 1.2 %convolution_convert_fusion = bf16[768,1152]{1,0:T(8,128)(2,1)S(1)} fusion(bf16[176,128]{1,0:T(8,128)(2,1)S(1)} %broadcast_multiply_fusion, bf16[176,1024]{1,0:T(8,128)(2,1)S(1)} %get-tuple-element.10, bf16[176,1024]{1,0:T(8,128)(2,1)S(1)} %get-tuple-element.9, s32[768]{0:T(1024)S(1)} %eq.48), kind=kOutput, calls=%fused_computation.4 | convolution fusion | flops 627253248 | bytes 2538496 | tf_op jit(solution)/shard_map/dot_general | solution.py:489
  47.5 19.4 %shard_map.111 = bf16[48,1152]{1,0:T(8,128)(2,1)S(1)} custom-call(bf16[16,48,1152]{2,1,0:T(8,128)(2,1)S(1)} %bitcast.10), custom_call_target="tpu_custom_call" | custom-call | tf_op jit(solution)/shard_map/pallas_call | solution.py:425
  67.1 0.6 select_reduce_fusion
  67.7 0.6 pad_maximum_fusion.1
  68.3 4.7 %fusion.35 = f32[2048,1024]{1,0:T(8,128)} fusion(bf16[176,1024]{1,0:T(8,128)(2,1)S(1)} %get-tuple-element.7, bf16[352,2048]{1,0:T(8,128)(2,1)S(1)} %copy-done.1), kind=kOutput, calls=%fused_computation.42 | convolution fusion | flops 738197504 | bytes 9469952 | tf_op jit(solution)/shard_map/dot_general | solution.py:31
  73.0 4.7 %fusion.33 = f32[2048,1024]{1,0:T(8,128)} fusion(bf16[176,1024]{1,0:T(8,128)(2,1)S(1)} %get-tuple-element.8, bf16[352,2048]{1,0:T(8,128)(2,1)S(1)} %copy-done.1), kind=kOutput, calls=%fused_computation.40 | convolution fusion | flops 738197504 | bytes 9469952 | tf_op jit(solution)/shard_map/dot_general | solution.py:34
  77.7 4.8 %fusion.22 = f32[1024,2048]{1,0:T(8,128)} fusion(bf16[176,1024]{1,0:T(8,128)(2,1)S(1)} %get-tuple-element.6, f32[176]{0:T(256)S(1)} %convert_element_type.127, bf16[352,2048]{1,0:T(8,128)(2,1)S(1)} %copy-done.1), kind=kOutput, calls=%fused_computation.22 | convolution fusion | flops 739278848 | bytes 9470976 | tf_op jit(solution)/shard_map/dot_general | solution.py:28
  (23 shorter events, 0.7 us)
Async XLA Ops:
  34.8 2.2 %copy-start.3 = (bf16[2048,1024]{1,0:T(8,128)(2,1)S(1)}, bf16[2048,1024]{1,0:T(8,128)(2,1)}, u32[]{:S(2)}) copy-start(bf16[2048,1024]{1,0:T(8,128)(2,1)} %param.11) | copy-start | bytes 12582916
  36.1 3.9 %copy-start = (bf16[352,2048]{1,0:T(8,128)(2,1)}, bf16[352,2048]{1,0:T(8,128)(2,1)S(1)}, u32[]{:S(2)}) copy-start(bf16[352,2048]{1,0:T(8,128)(2,1)S(1)} %fusion.6) | copy-start | bytes 4325380
  36.1 2.9 %copy-start.2 = (bf16[2048,1024]{1,0:T(8,128)(2,1)S(1)}, bf16[2048,1024]{1,0:T(8,128)(2,1)}, u32[]{:S(2)}) copy-start(bf16[2048,1024]{1,0:T(8,128)(2,1)} %param.12) | copy-start | bytes 12582916
  39.1 2.2 %copy-start.5 = (bf16[1024,2048]{1,0:T(8,128)(2,1)S(1)}, bf16[1024,2048]{1,0:T(8,128)(2,1)}, u32[]{:S(2)}) copy-start(bf16[1024,2048]{1,0:T(8,128)(2,1)} %param.13) | copy-start | bytes 12582916
  46.3 20.8 %copy-start.4 = (s32[24,6]{0,1:T(8,128)S(1)}, s32[24,6]{0,1:T(8,128)}, u32[]{:S(2)}) copy-start(s32[24,6]{0,1:T(8,128)} %param.9) | copy-start | bytes 1732
  46.3 22.0 %copy-start.1 = (bf16[352,2048]{1,0:T(8,128)(2,1)S(1)}, bf16[352,2048]{1,0:T(8,128)(2,1)}, u32[]{:S(2)}) copy-start(bf16[352,2048]{1,0:T(8,128)(2,1)} %copy-done) | copy-start | bytes 4325380

commit v4 on v3

--- a/solution.py
+++ b/solution.py
@@ -6,7 +6,44 @@
 from jax.sharding import PartitionSpec as P
 
 
-def expert_backward(row_tokens, row_cotan, row_mix, gate_matrix, up_matrix, down_matrix):
+def weight_kernel(x_ref, gate_ref, up_ref, hidden_ref, cotan_ref, dgate_ref, dup_ref, ddown_ref):
+    contract_first = (((0,), (0,)), ((), ()))
+    for left, right, out in (
+        (x_ref, gate_ref, dgate_ref),
+        (x_ref, up_ref, dup_ref),
+        (hidden_ref, cotan_ref, ddown_ref),
+    ):
+        out[...] = lax.dot_general(
+            left[...], right[...], contract_first, preferred_element_type=jnp.float32
+        )
+
+
+def weight_grads(rows_x, rows_gate, rows_up, rows_hidden, rows_cotan):
+    rows, features = rows_x.shape
+    units = rows_hidden.shape[1]
+    steps = 8
+    whole = lambda width: pl.BlockSpec((rows, width), lambda i: (0, 0))
+    piece = lambda width: pl.BlockSpec((rows, width // steps), lambda i: (0, i))
+    result = lambda height, width: pl.BlockSpec((height // steps, width), lambda i: (i, 0))
+    shape = lambda height, width: jax.ShapeDtypeStruct((height, width), jnp.float32)
+    return pl.pallas_call(
+        weight_kernel,
+        grid=(steps,),
+        in_specs=[piece(features), whole(units), whole(units), piece(units), whole(features)],
+        out_specs=[result(features, units), result(features, units), result(units, features)],
+        out_shape=[shape(features, units), shape(features, units), shape(units, features)],
+        compiler_params=pltpu.CompilerParams(vmem_limit_bytes=32 * 1024 * 1024),
+        cost_estimate=pl.CostEstimate(
+            flops=6 * rows * features * units,
+            bytes_accessed=12 * features * units,
+            transcendentals=0,
+        ),
+    )(rows_x, rows_gate, rows_up, rows_hidden, rows_cotan)
+
+
+def expert_backward(
+    row_tokens, row_cotan, row_mix, gate_matrix, up_matrix, down_matrix, tiled=False
+):
     contract_last = (((1,), (1,)), ((), ()))
     contract_first = (((0,), (0,)), ((), ()))
     pre_gate = jnp.dot(row_tokens, gate_matrix, preferred_element_type=jnp.float32)
@@ -25,15 +62,20 @@
         grad_hidden * pre_up * sigmoid_gate * (1.0 + pre_gate * (1.0 - sigmoid_gate))
     ).astype(jnp.bfloat16)
     mix_partial = jnp.sum(hidden.astype(jnp.float32) * back_hidden, axis=1).astype(jnp.bfloat16)
-    down_grad = lax.dot_general(
-        hidden, scaled_cotan, contract_first, preferred_element_type=jnp.float32
-    )
-    gate_grad = lax.dot_general(
-        row_tokens, grad_pregate, contract_first, preferred_element_type=jnp.float32
-    )
-    up_grad = lax.dot_general(
-        row_tokens, grad_upper, contract_first, preferred_element_type=jnp.float32
-    )
+    if tiled:
+        gate_grad, up_grad, down_grad = weight_grads(
+            row_tokens, grad_pregate, grad_upper, hidden, scaled_cotan
+        )
+    else:
+        down_grad = lax.dot_general(
+            hidden, scaled_cotan, contract_first, preferred_element_type=jnp.float32
+        )
+        gate_grad = lax.dot_general(
+            row_tokens, grad_pregate, contract_first, preferred_element_type=jnp.float32
+        )
+        up_grad = lax.dot_general(
+            row_tokens, grad_upper, contract_first, preferred_element_type=jnp.float32
+        )
     joined_grad = jnp.concatenate([grad_pregate, grad_upper], axis=1)
     joined_weight = jnp.concatenate([gate_matrix, up_matrix], axis=1)
     token_partial = lax.dot_general(
@@ -475,7 +517,7 @@
     weight_both = jnp.pad(weight, ((0, 0), (0, tok_count))).reshape(-1)
     row_mix = jnp.sum(pick[:rows].astype(f32) * weight_both[None, :], axis=1).astype(bf16)
     token_partial, mix_partial, gate_grad, up_grad, down_grad = expert_backward(
-        row_both[:rows], row_both[rows:], row_mix, gate_matrix, up_matrix, down_matrix
+        row_both[:rows], row_both[rows:], row_mix, gate_matrix, up_matrix, down_matrix, tiled=True
     )
     lane = (jnp.arange(128, dtype=jnp.int32)[None, :] == mine).astype(bf16)
     half = features // 2

time: 82.8 us -> 80.2 us (0.969)
  matrix products: 23.5 us -> 9.26 us
  Pallas kernels: 50 us -> 59.3 us
  other arithmetic: 4.1 us -> 5.91 us
    dot_general x3 -> x0, matrix products: 14.1 us -> none  [the longest x1 4.76 us: expert_backward(): lax.dot_general(hidden, scaled_cotan, contract_first, preferred_element_t...]
    pallas_call x0 -> x1, Pallas kernels: none -> 9.48 us  [weight_grads(): pl.pallas_call(weight_kernel, grid=(steps,), in_specs=[piece(features), w...]
    reduce_sum x1, other arithmetic: 0.15 us -> 1.06 us  [local_gather(): jnp.sum(pick[:rows].astype(f32) * weight_both[None, :], axis=1).astype(bf16)]
    unnamed x13 -> x9, local copies, waits for them, and re-layouts: 3.68 us -> 4.17 us
where the time goes in v4:
time: 80.2 us; the launch traced here: 79.9 us
  Pallas kernels  59.3 us (74%)
  matrix products  9.26 us (12%)
  other arithmetic  5.91 us (7%)
  local copies, waits for them, and re-layouts  4.62 us (6%)
    pallas_call x1, Pallas kernels, gather(): pl.pallas_call(lambda *refs: gather_kernel(height, *refs), out_shape=jax....  30.6 us
    pallas_call x1, Pallas kernels, scatter_sum(): pl.pallas_call(lambda *refs: reduce_kernel(height, *refs), out_shape=jax....  19.2 us
    pallas_call x1, Pallas kernels, weight_grads(): pl.pallas_call(weight_kernel, grid=(steps,), in_specs=[piece(features), w...  9.48 us
    unnamed x9, local copies, waits for them, and re-layouts  4.17 us
    dot_general x1, matrix products, expert_backward(): lax.dot_general(joined_grad, joined_weight, contract_last, preferred_elem...  2.93 us
    dot_general x1, matrix products, expert_backward(): lax.dot_general(row_cotan, down_matrix, contract_last, preferred_element_...  1.89 us

profile of v4, /device:TPU:1, one launch (start us, length us, event | category | flops | bytes accessed | tf_op | source)
XLA Modules:
  0.0 79.9 jit_solution(3333725670782560145)
XLA Ops:
  0.6 0.7 convert_element_type.86
  1.3 0.1 copy.18
  1.4 0.8 copy.19
  2.3 1.0 %pad_maximum_fusion.refs_0_ = bf16[48,2176]{1,0:T(8,128)(2,1)S(1)} fusion(bf16[48,128]{1,0:T(8,128)(2,1)S(1)} %fusion.36, bf16[24,2048]{1,0:T(8,128)(2,1)} %param.8, bf16[24,2048]{1,0:T(8,128)(2,1)} %param.7), kind=kLoop, calls=%fused_computation.38 | loop fusion | flops 626688 | bytes 417792 | tf_op jit(solution)/shard_map/concatenate | solution.py:498
  3.3 30.6 %shard_map.110 = bf16[16,48,2176]{2,1,0:T(8,128)(2,1)S(1)} custom-call(bf16[48,2176]{1,0:T(8,128)(2,1)S(1)} %pad_maximum_fusion.refs_0_), custom_call_target="tpu_custom_call" | custom-call | tf_op jit(solution)/shard_map/pallas_call | solution.py:337
  33.8 0.4 fusion.37
  34.3 0.1 pad_add_fusion
  34.5 0.9 %iota_compare_fusion.1 = pred[352,768]{1,0:T(8,128)(4,1)} fusion(s32[768]{0:T(1024)S(1)} %eq.48), kind=kLoop, calls=%fused_computation.15 | loop fusion | flops 270336 | bytes 273408 | tf_op jit(solution)/shard_map/eq | solution.py:514
  35.4 0.2 convert_reduce_fusion
  35.7 1.1 %multiply_reduce_fusion.1 = bf16[176]{0:T(256)(128)(2,1)S(1)} fusion(pred[352,768]{1,0:T(8,128)(4,1)} %iota_compare_fusion.1, f32[768]{0:T(1024)S(1)} %mul.76), kind=kLoop, calls=%fused_computation.33 | loop fusion | flops 540496 | bytes 138592 | tf_op jit(solution)/shard_map/reduce_sum | solution.py:518
  36.7 1.3 %fusion.6 = bf16[352,2048]{1,0:T(8,128)(2,1)S(1)} fusion(bf16[768,2176]{1,0:T(8,128)(2,1)S(1)} %bitcast.6, s32[768]{0:T(1024)S(1)} %eq.48), kind=kOutput, calls=%fused_computation.7 | convolution fusion | flops 1108287488 | bytes 4591616 | tf_op jit(solution)/shard_map/dot_general | solution.py:516
  38.0 0.9 %copy-done.1 = bf16[2048,1024]{1,0:T(8,128)(2,1)S(1)} copy-done((bf16[2048,1024]{1,0:T(8,128)(2,1)S(1)}, bf16[2048,1024]{1,0:T(8,128)(2,1)}, u32[]{:S(2)}) %copy-start.1) | copy-done | bytes 4194328
  38.9 0.9 %fusion.42 = f32[176,1024]{1,0:T(8,128)S(1)} fusion(bf16[2048,1024]{1,0:T(8,128)(2,1)S(1)} %copy-done.1, bf16[352,2048]{1,0:T(8,128)(2,1)S(1)} %fusion.6), kind=kOutput, calls=%fused_computation.65 | convolution fusion | flops 738197504 | bytes 5636096 | tf_op jit(solution)/shard_map/dot_general | solution.py:49
  39.9 1.3 %copy-done = bf16[2048,1024]{1,0:T(8,128)(2,1)S(1)} copy-done((bf16[2048,1024]{1,0:T(8,128)(2,1)S(1)}, bf16[2048,1024]{1,0:T(8,128)(2,1)}, u32[]{:S(2)}) %copy-start) | copy-done | bytes 4194328
  41.1 0.9 %fusion.44 = f32[176,1024]{1,0:T(8,128)S(1)} fusion(bf16[2048,1024]{1,0:T(8,128)(2,1)S(1)} %copy-done, bf16[352,2048]{1,0:T(8,128)(2,1)S(1)} %fusion.6), kind=kOutput, calls=%fused_computation.67 | convolution fusion | flops 738197504 | bytes 5636096 | tf_op jit(solution)/shard_map/dot_general | solution.py:50
  42.0 1.3 %copy-done.3 = bf16[1024,2048]{1,0:T(8,128)(2,1)S(1)} copy-done((bf16[1024,2048]{1,0:T(8,128)(2,1)S(1)}, bf16[1024,2048]{1,0:T(8,128)(2,1)}, u32[]{:S(2)}) %copy-start.3) | copy-done | bytes 4194328
  43.3 1.9 %multiply_reduce_fusion = (bf16[176]{0:T(256)(128)(2,1)S(1)}, bf16[176,1024]{1,0:T(8,128)(2,1)S(1)}, bf16[176,1024]{1,0:T(8,128)(2,1)S(1)}, bf16[176,1024]{1,0:T(8,128)(2,1)S(1)}) fusion(f32[176,1024]{1,0:T(8,128)S(1)} %fusion.44, f32[176,1024]{1,0:T(8,128)S(1)} %fusion.42, f32[176]{0:T(256)S(1)} %convert_element_type.125, ...), kind=kOutput, calls=%fused_computation.25 | convolution fusion | flops 741621568 | bytes 7439712 | tf_op jit(solution)/shard_map/dot_general | solution.py:54
  45.2 0.2 multiply_convert_fusion.cotan_ref
  45.5 9.5 %shard_map.112 = (f32[2048,1024]{1,0:T(8,128)}, f32[2048,1024]{1,0:T(8,128)}, f32[1024,2048]{1,0:T(8,128)}) custom-call(bf16[176,2048]{1,0:T(8,128)(2,1)S(1)} %slice.51.x_ref, bf16[176,1024]{1,0:T(8,128)(2,1)S(1)} %get-tuple-element.13.gate_ref, bf16[176,1024]{1,0:T(8,128)(2,1)S(1)} %get-tuple-element.14.up_ref, ...), custom_call_target="tpu_custom_call" | custom-call | flops 2214592512 | bytes 25165824 | tf_op jit(solution)/shard_map/pallas_call | solution.py:29
  54.9 2.9 %fusion.9 = bf16[176,2048]{1,0:T(8,128)(2,1)S(1)} fusion(bf16[2048,1024]{1,0:T(8,128)(2,1)S(1)} %copy-done, bf16[2048,1024]{1,0:T(8,128)(2,1)S(1)} %copy-done.1, bf16[176,1024]{1,0:T(8,128)(2,1)S(1)} %get-tuple-element.14.up_ref, bf16[176,1024]{1,0:T(8,128)(2,1)S(1)} %get-tuple-element.13.gate_ref), kind=kOutput, calls=%fused_computation.8 | convolution fusion | flops 1494974464 | bytes 9830400 | tf_op jit(solution)/shard_map/dot_general | solution.py:81
  58.0 1.2 %convolution_convert_fusion = bf16[768,1152]{1,0:T(8,128)(2,1)S(1)} fusion(bf16[176,128]{1,0:T(8,128)(2,1)S(1)} %broadcast_multiply_fusion, bf16[176,1024]{1,0:T(8,128)(2,1)S(1)} %get-tuple-element.16, bf16[176,1024]{1,0:T(8,128)(2,1)S(1)} %get-tuple-element.15, s32[768]{0:T(1024)S(1)} %eq.48), kind=kOutput, calls=%fused_computation.4 | convolution fusion | flops 627253248 | bytes 2538496 | tf_op jit(solution)/shard_map/dot_general | solution.py:531
  59.3 19.2 %shard_map.111 = bf16[48,1152]{1,0:T(8,128)(2,1)S(1)} custom-call(bf16[16,48,1152]{2,1,0:T(8,128)(2,1)S(1)} %bitcast.7), custom_call_target="tpu_custom_call" | custom-call | tf_op jit(solution)/shard_map/pallas_call | solution.py:467
  78.5 0.6 pad_maximum_fusion.1
  79.3 0.6 select_reduce_fusion
  (19 shorter events, 0.6 us)
Async XLA Ops:
  36.7 2.2 %copy-start.1 = (bf16[2048,1024]{1,0:T(8,128)(2,1)S(1)}, bf16[2048,1024]{1,0:T(8,128)(2,1)}, u32[]{:S(2)}) copy-start(bf16[2048,1024]{1,0:T(8,128)(2,1)} %param.11) | copy-start | bytes 12582916
  38.9 2.2 %copy-start = (bf16[2048,1024]{1,0:T(8,128)(2,1)S(1)}, bf16[2048,1024]{1,0:T(8,128)(2,1)}, u32[]{:S(2)}) copy-start(bf16[2048,1024]{1,0:T(8,128)(2,1)} %param.12) | copy-start | bytes 12582916
  41.1 2.2 %copy-start.3 = (bf16[1024,2048]{1,0:T(8,128)(2,1)S(1)}, bf16[1024,2048]{1,0:T(8,128)(2,1)}, u32[]{:S(2)}) copy-start(bf16[1024,2048]{1,0:T(8,128)(2,1)} %param.13) | copy-start | bytes 12582916
  58.0 21.2 %copy-start.2 = (s32[24,6]{0,1:T(8,128)S(1)}, s32[24,6]{0,1:T(8,128)}, u32[]{:S(2)}) copy-start(s32[24,6]{0,1:T(8,128)} %param.9) | copy-start | bytes 1732
